TPU v7x, 32 devices: a whole 2x2x4 slice. The times are simulated.
32 devices in a mesh: row: 4 (over y, x), col: 8 (over z, core).
Axes of the slice: x: 2, y: 2, z: 4, core: 2. Of those that a mesh axis runs over, the one named last changes fastest.
Arguments:
- start_block: float32 [32, 12288], P(None, ('row', 'col')), may hold values from -6 to 6
- center: float32 [1], replicated, may hold values from 1.05 to 1.15
- half_width: float32 [1], replicated, may hold values from 0.85 to 0.95
- matrix_tiles: bfloat16 [4, 384, 192, 192], P('row', 'col')
- tile_row: int32 [4, 384], P('row', 'col'), may hold values from 0 to 15, as said below
- tile_col: int32 [4, 384], P('row', 'col'), may hold values from 0 to 7, as said below
- tile_live: int32 [4, 384], P('row', 'col'), may hold values from 0 to 1
Outputs:
- filtered: float32 [32, 12288], P(None, ('row', 'col'))
- previous: float32 [32, 12288], P(None, ('row', 'col'))
Inputs may be any that keep to these rules, and one draw needn't show every extreme that they name: tile_row lies within the device's row clusters; on a live slot the block row's atom order is at most the block column's. tile_col lies within the device's column clusters.
All inputs are finite; a program needn't handle non-finite values.
Results may differ from a plain program's by a relative error of at most 0.03.
Values may be sent and summed in bfloat16 or wider, within the bound.
A program may use at most 64 MiB of HBM per device.

v0:
```python
import jax
import jax.numpy as jnp
from jax import lax
from jax.sharding import PartitionSpec as P

DEG = 8


def spread(block, axis, source):
    block = jnp.where(lax.axis_index(axis) == source, block, jnp.zeros_like(block))
    return lax.psum(block, axis)


def advance(degree, product, current, earlier, center_value, half_value):
    if degree == 0:
        return (product - center_value * current) / half_value
    return 2.0 * (product - center_value * current) / half_value - earlier


def body(start_block, center, half_width, matrix_tiles, tile_row, tile_col, tile_live):
    tile_size = matrix_tiles.shape[-1]
    vector_count = start_block.shape[0]
    own_clusters = start_block.shape[1] // tile_size
    row_count = lax.axis_size("row")
    col_count = lax.axis_size("col")
    panel_rows = own_clusters * col_count
    panel_cols = own_clusters * row_count
    row_index = lax.axis_index("row")
    col_index = lax.axis_index("col")
    root_row = col_index * row_count // col_count
    offset = col_index * row_count % col_count * own_clusters
    owner_flag = (row_index == root_row).astype(jnp.float32)
    center_value = center[0]
    half_value = half_width[0]
    stored = matrix_tiles[0]
    row_ids = tile_row[0]
    col_ids = tile_col[0]
    weights = tile_live[0].astype(jnp.float32)
    row_onehot = (row_ids[:, None] == jnp.arange(panel_rows, dtype=jnp.int32)[None, :]).astype(
        jnp.float32
    ) * weights[:, None]
    col_onehot = (col_ids[:, None] == jnp.arange(panel_cols, dtype=jnp.int32)[None, :]).astype(
        jnp.float32
    ) * weights[:, None]
    highest = lax.Precision.HIGHEST
    own_vectors = start_block.reshape(vector_count, own_clusters, tile_size)
    current = own_vectors
    earlier = current
    for degree in range(DEG):
        row_panel = lax.all_gather(current.astype(jnp.bfloat16), "col", axis=1, tiled=True)
        col_source = lax.dynamic_slice_in_dim(row_panel, offset, panel_cols, 1)
        col_panel = spread(col_source, "row", root_row)
        x_col = jnp.take(col_panel, col_ids, axis=1)
        direct = jnp.einsum("ksb,sab->ksa", x_col, stored, preferred_element_type=jnp.float32)
        row_part = jnp.einsum("ksa,sr->kra", direct, row_onehot, precision=highest)
        x_row = jnp.take(row_panel, row_ids, axis=1)
        mirrored = jnp.einsum("ksa,sab->ksb", x_row, stored, preferred_element_type=jnp.float32)
        mirror_part = jnp.einsum("ksb,sc->kcb", mirrored, col_onehot, precision=highest)
        mirror_total = lax.psum(mirror_part, "row")
        placed = lax.dynamic_update_slice_in_dim(
            jnp.zeros_like(row_part), mirror_total * owner_flag, offset, 1
        )
        partial_sum = row_part + placed
        product = lax.psum_scatter(partial_sum, "col", scatter_dimension=1, tiled=True)
        following = advance(degree, product, current, earlier, center_value, half_value)
        earlier, current = (current, following)
    flat_shape = (vector_count, own_clusters * tile_size)
    return (current.reshape(flat_shape), earlier.reshape(flat_shape))


def solution(mesh):
    in_specs = (
        P(None, ("row", "col")),
        P(),
        P(),
        P("row", "col", None, None),
        P("row", "col"),
        P("row", "col"),
        P("row", "col"),
    )
    out_specs = (P(None, ("row", "col")), P(None, ("row", "col")))
    return jax.shard_map(body, mesh=mesh, in_specs=in_specs, out_specs=out_specs, check_vma=False)
```

profile of v0, /device:TPU:6, one launch (start us, length us, event | category | flops | bytes accessed | tf_op | source)
XLA Modules:
  0.0 1108.6 jit_solution(9567063673831491790)
XLA Ops:
  8.2 14.4 %all_gather.24 = bf16[32,16,192]{2,0,1:T(8,128)(2,1)S(1)} all-gather(bf16[32,2,192]{2,0,1:T(8,128)(2,1)S(1)} %copy.89), channel_id=1, replica_groups=mesh['row'=4,'col'=8] {'col'}, dimensions={1}, use_global_device_ids=true | all-gather | bytes 221184 | tf_op jit(solution)/shard_map/all_gather | solution.py:50
  26.0 3.4 fusion.67
  29.3 2.4 fusion.112
  31.9 33.7 %all-reduce.17.cloned.1.call-done = bf16[32,8,192]{2,0,1:T(8,128)(2,1)} async-done(((bf16[32,8,192]{2,0,1:T(8,128)(2,1)}), bf16[32,8,192]{2,0,1:T(8,128)(2,1)}) %all-reduce.17.cloned.1.call-update) | async-done | bytes 98320 | tf_op jit(solution)/shard_map/psum | solution.py:11
  67.1 3.9 fusion.64
  71.0 1.7 fusion.62
  72.7 39.0 %all-reduce.19.cloned.1.call-done = f32[32,8,192]{2,1,0:T(8,128)} async-done(((f32[32,8,192]{2,1,0:T(8,128)}), f32[32,8,192]{2,1,0:T(8,128)}) %all-reduce.19.cloned.1.call-update) | async-done | bytes 196624 | tf_op jit(solution)/shard_map/psum | solution.py:59
  115.5 30.7 %reduce-scatter.9.cloned.1.call-done = f32[32,2,192]{2,0,1:T(8,128)} async-done(((f32[32,16,192]{2,0,1:T(8,128)}), f32[32,2,192]{2,0,1:T(8,128)}) %reduce-scatter.9.cloned.1.call-update) | async-done | bytes 49168 | tf_op jit(solution)/shard_map/reduce_scatter | solution.py:64
  147.1 14.2 %all_gather.25 = bf16[32,16,192]{2,0,1:T(8,128)(2,1)S(1)} all-gather(bf16[32,2,192]{2,0,1:T(8,128)(2,1)S(1)} %fusion.312), channel_id=1, replica_groups=mesh['row'=4,'col'=8] {'col'}, dimensions={1}, use_global_device_ids=true | all-gather | bytes 221184 | tf_op jit(solution)/shard_map/all_gather | solution.py:50
  162.6 3.3 fusion.73
  166.0 2.4 fusion.115
  169.0 33.1 %all-reduce.21.cloned.1.call-done = bf16[32,8,192]{2,0,1:T(8,128)(2,1)} async-done(((bf16[32,8,192]{2,0,1:T(8,128)(2,1)}), bf16[32,8,192]{2,0,1:T(8,128)(2,1)}) %all-reduce.21.cloned.1.call-update) | async-done | bytes 98320 | tf_op jit(solution)/shard_map/psum | solution.py:11
  203.5 3.9 fusion.70
  207.4 1.7 fusion.58
  209.2 38.6 %all-reduce.23.cloned.1.call-done = f32[32,8,192]{2,1,0:T(8,128)} async-done(((f32[32,8,192]{2,1,0:T(8,128)}), f32[32,8,192]{2,1,0:T(8,128)}) %all-reduce.23.cloned.1.call-update) | async-done | bytes 196624 | tf_op jit(solution)/shard_map/psum | solution.py:59
  250.3 31.9 %reduce-scatter.11.cloned.1.call-done = f32[32,2,192]{2,0,1:T(8,128)} async-done(((f32[32,16,192]{2,0,1:T(8,128)}), f32[32,2,192]{2,0,1:T(8,128)}) %reduce-scatter.11.cloned.1.call-update) | async-done | bytes 49168 | tf_op jit(solution)/shard_map/reduce_scatter | solution.py:64
  283.1 14.2 %all_gather.26 = bf16[32,16,192]{2,0,1:T(8,128)(2,1)S(1)} all-gather(bf16[32,2,192]{2,0,1:T(8,128)(2,1)S(1)} %get-tuple-element.14), channel_id=1, replica_groups=mesh['row'=4,'col'=8] {'col'}, dimensions={1}, use_global_device_ids=true | all-gather | bytes 221184 | tf_op jit(solution)/shard_map/all_gather | solution.py:50
  298.6 3.3 fusion.79
  302.0 2.4 fusion.118
  304.5 33.6 %all-reduce.25.cloned.1.call-done = bf16[32,8,192]{2,0,1:T(8,128)(2,1)} async-done(((bf16[32,8,192]{2,0,1:T(8,128)(2,1)}), bf16[32,8,192]{2,0,1:T(8,128)(2,1)}) %all-reduce.25.cloned.1.call-update) | async-done | bytes 98320 | tf_op jit(solution)/shard_map/psum | solution.py:11
  339.6 3.9 fusion.76
  343.4 1.7 fusion.54
  345.2 39.0 %all-reduce.27.cloned.1.call-done = f32[32,8,192]{2,1,0:T(8,128)} async-done(((f32[32,8,192]{2,1,0:T(8,128)}), f32[32,8,192]{2,1,0:T(8,128)}) %all-reduce.27.cloned.1.call-update) | async-done | bytes 196624 | tf_op jit(solution)/shard_map/psum | solution.py:59
  386.7 32.0 %reduce-scatter.13.cloned.1.call-done = f32[32,2,192]{2,0,1:T(8,128)} async-done(((f32[32,16,192]{2,0,1:T(8,128)}), f32[32,2,192]{2,0,1:T(8,128)}) %reduce-scatter.13.cloned.1.call-update) | async-done | bytes 49168 | tf_op jit(solution)/shard_map/reduce_scatter | solution.py:64
  419.5 14.2 %all_gather.27 = bf16[32,16,192]{2,0,1:T(8,128)(2,1)S(1)} all-gather(bf16[32,2,192]{2,0,1:T(8,128)(2,1)S(1)} %get-tuple-element.12), channel_id=1, replica_groups=mesh['row'=4,'col'=8] {'col'}, dimensions={1}, use_global_device_ids=true | all-gather | bytes 221184 | tf_op jit(solution)/shard_map/all_gather | solution.py:50
  435.3 3.3 fusion.85
  438.6 2.4 fusion.121
  441.1 33.4 %all-reduce.29.cloned.1.call-done = bf16[32,8,192]{2,0,1:T(8,128)(2,1)} async-done(((bf16[32,8,192]{2,0,1:T(8,128)(2,1)}), bf16[32,8,192]{2,0,1:T(8,128)(2,1)}) %all-reduce.29.cloned.1.call-update) | async-done | bytes 98320 | tf_op jit(solution)/shard_map/psum | solution.py:11
  476.0 3.9 fusion.82
  479.9 1.7 fusion.50
  481.6 38.8 %all-reduce.31.cloned.1.call-done = f32[32,8,192]{2,1,0:T(8,128)} async-done(((f32[32,8,192]{2,1,0:T(8,128)}), f32[32,8,192]{2,1,0:T(8,128)}) %all-reduce.31.cloned.1.call-update) | async-done | bytes 196624 | tf_op jit(solution)/shard_map/psum | solution.py:59
  522.9 31.9 %reduce-scatter.15.cloned.1.call-done = f32[32,2,192]{2,0,1:T(8,128)} async-done(((f32[32,16,192]{2,0,1:T(8,128)}), f32[32,2,192]{2,0,1:T(8,128)}) %reduce-scatter.15.cloned.1.call-update) | async-done | bytes 49168 | tf_op jit(solution)/shard_map/reduce_scatter | solution.py:64
  555.7 14.2 %all_gather.28 = bf16[32,16,192]{2,0,1:T(8,128)(2,1)S(1)} all-gather(bf16[32,2,192]{2,0,1:T(8,128)(2,1)S(1)} %get-tuple-element.10), channel_id=1, replica_groups=mesh['row'=4,'col'=8] {'col'}, dimensions={1}, use_global_device_ids=true | all-gather | bytes 221184 | tf_op jit(solution)/shard_map/all_gather | solution.py:50
  571.2 3.3 fusion.91
  574.6 2.4 fusion.124
  577.3 33.4 %all-reduce.33.cloned.1.call-done = bf16[32,8,192]{2,0,1:T(8,128)(2,1)} async-done(((bf16[32,8,192]{2,0,1:T(8,128)(2,1)}), bf16[32,8,192]{2,0,1:T(8,128)(2,1)}) %all-reduce.33.cloned.1.call-update) | async-done | bytes 98320 | tf_op jit(solution)/shard_map/psum | solution.py:11
  612.2 3.9 fusion.88
  616.1 1.7 fusion.46
  617.8 38.9 %all-reduce.35.cloned.1.call-done = f32[32,8,192]{2,1,0:T(8,128)} async-done(((f32[32,8,192]{2,1,0:T(8,128)}), f32[32,8,192]{2,1,0:T(8,128)}) %all-reduce.35.cloned.1.call-update) | async-done | bytes 196624 | tf_op jit(solution)/shard_map/psum | solution.py:59
  659.1 32.0 %reduce-scatter.17.cloned.1.call-done = f32[32,2,192]{2,0,1:T(8,128)} async-done(((f32[32,16,192]{2,0,1:T(8,128)}), f32[32,2,192]{2,0,1:T(8,128)}) %reduce-scatter.17.cloned.1.call-update) | async-done | bytes 49168 | tf_op jit(solution)/shard_map/reduce_scatter | solution.py:64
  692.0 14.2 %all_gather.29 = bf16[32,16,192]{2,0,1:T(8,128)(2,1)S(1)} all-gather(bf16[32,2,192]{2,0,1:T(8,128)(2,1)S(1)} %get-tuple-element.8), channel_id=1, replica_groups=mesh['row'=4,'col'=8] {'col'}, dimensions={1}, use_global_device_ids=true | all-gather | bytes 221184 | tf_op jit(solution)/shard_map/all_gather | solution.py:50
  707.6 3.3 fusion.97
  710.9 2.4 fusion.127
  713.4 33.6 %all-reduce.37.cloned.1.call-done = bf16[32,8,192]{2,0,1:T(8,128)(2,1)} async-done(((bf16[32,8,192]{2,0,1:T(8,128)(2,1)}), bf16[32,8,192]{2,0,1:T(8,128)(2,1)}) %all-reduce.37.cloned.1.call-update) | async-done | bytes 98320 | tf_op jit(solution)/shard_map/psum | solution.py:11
  748.5 3.9 fusion.94
  752.4 1.7 fusion.42
  754.1 38.6 %all-reduce.39.cloned.1.call-done = f32[32,8,192]{2,1,0:T(8,128)} async-done(((f32[32,8,192]{2,1,0:T(8,128)}), f32[32,8,192]{2,1,0:T(8,128)}) %all-reduce.39.cloned.1.call-update) | async-done | bytes 196624 | tf_op jit(solution)/shard_map/psum | solution.py:59
  795.2 31.9 %reduce-scatter.19.cloned.1.call-done = f32[32,2,192]{2,0,1:T(8,128)} async-done(((f32[32,16,192]{2,0,1:T(8,128)}), f32[32,2,192]{2,0,1:T(8,128)}) %reduce-scatter.19.cloned.1.call-update) | async-done | bytes 49168 | tf_op jit(solution)/shard_map/reduce_scatter | solution.py:64
  828.0 14.2 %all_gather.30 = bf16[32,16,192]{2,0,1:T(8,128)(2,1)S(1)} all-gather(bf16[32,2,192]{2,0,1:T(8,128)(2,1)S(1)} %get-tuple-element.6), channel_id=1, replica_groups=mesh['row'=4,'col'=8] {'col'}, dimensions={1}, use_global_device_ids=true | all-gather | bytes 221184 | tf_op jit(solution)/shard_map/all_gather | solution.py:50
  843.8 3.3 fusion.103
  847.2 2.4 fusion.130
  849.6 33.3 %all-reduce.41.cloned.1.call-done = bf16[32,8,192]{2,0,1:T(8,128)(2,1)} async-done(((bf16[32,8,192]{2,0,1:T(8,128)(2,1)}), bf16[32,8,192]{2,0,1:T(8,128)(2,1)}) %all-reduce.41.cloned.1.call-update) | async-done | bytes 98320 | tf_op jit(solution)/shard_map/psum | solution.py:11
  884.5 3.9 fusion.100
  888.4 1.7 fusion.38
  890.1 38.9 %all-reduce.43.cloned.1.call-done = f32[32,8,192]{2,1,0:T(8,128)} async-done(((f32[32,8,192]{2,1,0:T(8,128)}), f32[32,8,192]{2,1,0:T(8,128)}) %all-reduce.43.cloned.1.call-update) | async-done | bytes 196624 | tf_op jit(solution)/shard_map/psum | solution.py:59
  931.4 32.0 %reduce-scatter.21.cloned.1.call-done = f32[32,2,192]{2,0,1:T(8,128)} async-done(((f32[32,16,192]{2,0,1:T(8,128)}), f32[32,2,192]{2,0,1:T(8,128)}) %reduce-scatter.21.cloned.1.call-update) | async-done | bytes 49168 | tf_op jit(solution)/shard_map/reduce_scatter | solution.py:64
  964.3 14.2 %all_gather.31 = bf16[32,16,192]{2,0,1:T(8,128)(2,1)S(1)} all-gather(bf16[32,2,192]{2,0,1:T(8,128)(2,1)S(1)} %get-tuple-element.4), channel_id=1, replica_groups=mesh['row'=4,'col'=8] {'col'}, dimensions={1}, use_global_device_ids=true | all-gather | bytes 221184 | tf_op jit(solution)/shard_map/all_gather | solution.py:50
  979.9 3.3 fusion.109
  983.2 2.4 fusion.133
  986.0 33.3 %all-reduce.45.cloned.1.call-done = bf16[32,8,192]{2,0,1:T(8,128)(2,1)} async-done(((bf16[32,8,192]{2,0,1:T(8,128)(2,1)}), bf16[32,8,192]{2,0,1:T(8,128)(2,1)}) %all-reduce.45.cloned.1.call-update) | async-done | bytes 98320 | tf_op jit(solution)/shard_map/psum | solution.py:11
  1020.8 3.9 fusion.106
  1024.7 1.7 fusion.34
  1026.4 38.8 %all-reduce.47.cloned.1.call-done = f32[32,8,192]{2,1,0:T(8,128)} async-done(((f32[32,8,192]{2,1,0:T(8,128)}), f32[32,8,192]{2,1,0:T(8,128)}) %all-reduce.47.cloned.1.call-update) | async-done | bytes 196624 | tf_op jit(solution)/shard_map/psum | solution.py:59
  1068.4 31.2 %reduce-scatter.23.cloned.1.call-done = f32[32,2,192]{2,0,1:T(8,128)} async-done(((f32[32,16,192]{2,0,1:T(8,128)}), f32[32,2,192]{2,0,1:T(8,128)}) %reduce-scatter.23.cloned.1.call-update) | async-done | bytes 49168 | tf_op jit(solution)/shard_map/reduce_scatter | solution.py:64
  (124 shorter events, 55.9 us)
Async XLA Ops:
  7.2 58.4 %all-reduce.17.cloned.1.call-start = ((), (), s32[]{:S(2)}) async-start(), calls=%async_computation.8 | async-start | bytes 262144 | tf_op jit(solution)/shard_map/psum | solution.py:11
  23.3 88.4 %all-reduce.19.cloned.1.call-start = ((), (), s32[]{:S(2)}) async-start(), calls=%async_computation.9 | async-start | bytes 524288 | tf_op jit(solution)/shard_map/psum | solution.py:59
  26.0 3.4 copy-start.1
  31.8 114.4 %reduce-scatter.9.cloned.1.call-start = ((), (), s32[]{:S(2)}) async-start(), calls=%async_computation.10 | async-start | bytes 589824 | tf_op jit(solution)/shard_map/reduce_scatter | solution.py:64
  67.1 3.9 copy-start.2
  114.1 87.9 %all-reduce.21.cloned.1.call-start = ((), (), s32[]{:S(2)}) async-start(), calls=%async_computation.11 | async-start | bytes 262144 | tf_op jit(solution)/shard_map/psum | solution.py:11
  162.6 85.2 %all-reduce.23.cloned.1.call-start = ((), (), s32[]{:S(2)}) async-start(), calls=%async_computation.12 | async-start | bytes 524288 | tf_op jit(solution)/shard_map/psum | solution.py:59
  168.4 113.8 %reduce-scatter.11.cloned.1.call-start = ((), (), s32[]{:S(2)}) async-start(), calls=%async_computation.13 | async-start | bytes 589824 | tf_op jit(solution)/shard_map/reduce_scatter | solution.py:64
  209.1 73.1 %copy-start = (f32[32,2,192]{2,0,1:T(8,128)S(1)}, f32[32,2,192]{2,0,1:T(8,128)}, u32[]{:S(2)}) copy-start(f32[32,2,192]{2,0,1:T(8,128)} %reduce-scatter.9.cloned.1.call-done) | copy-start | bytes 147460
  250.2 87.8 %all-reduce.25.cloned.1.call-start = ((), (), s32[]{:S(2)}) async-start(), calls=%async_computation.14 | async-start | bytes 262144 | tf_op jit(solution)/shard_map/psum | solution.py:11
  298.6 85.6 %all-reduce.27.cloned.1.call-start = ((), (), s32[]{:S(2)}) async-start(), calls=%async_computation.15 | async-start | bytes 524288 | tf_op jit(solution)/shard_map/psum | solution.py:59
  304.4 114.3 %reduce-scatter.13.cloned.1.call-start = ((), (), s32[]{:S(2)}) async-start(), calls=%async_computation.16 | async-start | bytes 589824 | tf_op jit(solution)/shard_map/reduce_scatter | solution.py:64
  386.6 87.9 %all-reduce.29.cloned.1.call-start = ((), (), s32[]{:S(2)}) async-start(), calls=%async_computation.17 | async-start | bytes 262144 | tf_op jit(solution)/shard_map/psum | solution.py:11
  435.0 85.4 %all-reduce.31.cloned.1.call-start = ((), (), s32[]{:S(2)}) async-start(), calls=%async_computation.18 | async-start | bytes 524288 | tf_op jit(solution)/shard_map/psum | solution.py:59
  441.0 113.8 %reduce-scatter.15.cloned.1.call-start = ((), (), s32[]{:S(2)}) async-start(), calls=%async_computation.19 | async-start | bytes 589824 | tf_op jit(solution)/shard_map/reduce_scatter | solution.py:64
  522.8 87.8 %all-reduce.33.cloned.1.call-start = ((), (), s32[]{:S(2)}) async-start(), calls=%async_computation.20 | async-start | bytes 262144 | tf_op jit(solution)/shard_map/psum | solution.py:11
  571.2 85.4 %all-reduce.35.cloned.1.call-start = ((), (), s32[]{:S(2)}) async-start(), calls=%async_computation.21 | async-start | bytes 524288 | tf_op jit(solution)/shard_map/psum | solution.py:59
  577.0 114.1 %reduce-scatter.17.cloned.1.call-start = ((), (), s32[]{:S(2)}) async-start(), calls=%async_computation.22 | async-start | bytes 589824 | tf_op jit(solution)/shard_map/reduce_scatter | solution.py:64
  659.1 87.9 %all-reduce.37.cloned.1.call-start = ((), (), s32[]{:S(2)}) async-start(), calls=%async_computation.23 | async-start | bytes 262144 | tf_op jit(solution)/shard_map/psum | solution.py:11
  707.5 85.2 %all-reduce.39.cloned.1.call-start = ((), (), s32[]{:S(2)}) async-start(), calls=%async_computation.24 | async-start | bytes 524288 | tf_op jit(solution)/shard_map/psum | solution.py:59
  713.3 113.8 %reduce-scatter.19.cloned.1.call-start = ((), (), s32[]{:S(2)}) async-start(), calls=%async_computation.25 | async-start | bytes 589824 | tf_op jit(solution)/shard_map/reduce_scatter | solution.py:64
  795.2 87.8 %all-reduce.41.cloned.1.call-start = ((), (), s32[]{:S(2)}) async-start(), calls=%async_computation.26 | async-start | bytes 262144 | tf_op jit(solution)/shard_map/psum | solution.py:11
  843.5 85.4 %all-reduce.43.cloned.1.call-start = ((), (), s32[]{:S(2)}) async-start(), calls=%async_computation.27 | async-start | bytes 524288 | tf_op jit(solution)/shard_map/psum | solution.py:59
  849.6 113.9 %reduce-scatter.21.cloned.1.call-start = ((), (), s32[]{:S(2)}) async-start(), calls=%async_computation.28 | async-start | bytes 589824 | tf_op jit(solution)/shard_map/reduce_scatter | solution.py:64
  931.4 87.9 %all-reduce.45.cloned.1.call-start = ((), (), s32[]{:S(2)}) async-start(), calls=%async_computation.29 | async-start | bytes 262144 | tf_op jit(solution)/shard_map/psum | solution.py:11
  979.8 85.4 %all-reduce.47.cloned.1.call-start = ((), (), s32[]{:S(2)}) async-start(), calls=%async_computation.30 | async-start | bytes 524288 | tf_op jit(solution)/shard_map/psum | solution.py:59
  985.6 114.0 %reduce-scatter.23.cloned.1.call-start = ((), (), s32[]{:S(2)}) async-start(), calls=%async_computation.31 | async-start | bytes 589824 | tf_op jit(solution)/shard_map/reduce_scatter | solution.py:64
Sparse Core Ops, SparseCore 0:
  23.4 42.0 all-reduce.16
  68.8 42.9 all-reduce.18
  114.3 31.8 reduce-scatter.8
  162.7 39.2 all-reduce.20
  204.8 42.9 all-reduce.22
  250.3 31.8 reduce-scatter.10
  298.7 39.2 all-reduce.24
  341.2 42.9 all-reduce.26
  386.7 31.8 reduce-scatter.12
  435.2 39.2 all-reduce.28
  477.4 42.9 all-reduce.30
  523.0 31.8 reduce-scatter.14
  571.3 39.2 all-reduce.32
  613.7 42.9 all-reduce.34
  659.2 31.8 reduce-scatter.16
  707.6 39.2 all-reduce.36
  749.7 42.9 all-reduce.38
  795.3 31.8 reduce-scatter.18
  843.6 39.2 all-reduce.40
  886.0 42.9 all-reduce.42
  931.5 31.8 reduce-scatter.20
  979.9 39.2 all-reduce.44
  1022.2 42.9 all-reduce.46
  1067.7 31.8 reduce-scatter.22
where the time goes:
time: 1120 us; the launch traced here: 1110 us
  waiting for transfers between devices  832 us (74%)
  blocking collectives  114 us (10%)
  matrix products  90.7 us (8%)
  local copies, waits for them, and re-layouts  30.8 us (3%)
  other arithmetic  22.2 us (2%)
  between operations  16.6 us (1%)
    psum x8, waiting for transfers between devices, body(): mirror_total = lax.psum(mirror_part, 'row')  310 us
    psum x8, waiting for transfers between devices, spread(): return lax.psum(block, axis)  267 us
    reduce_scatter x8, waiting for transfers between devices, body(): lax.psum_scatter(partial_sum, 'col', scatter_dimension=1, tiled=True)  254 us
    all_gather x8, blocking collectives, body(): lax.all_gather(current.astype(jnp.bfloat16), 'col', axis=1, tiled=True)  114 us
    dot_general x8, matrix products, body(): jnp.einsum('ksb,sab->ksa', x_col, stored, preferred_element_type=jnp.floa...  31 us
    dot_general x8, matrix products, body(): jnp.einsum('ksa,sab->ksb', x_row, stored, preferred_element_type=jnp.floa...  26.8 us
  transfers between devices with their start and end apart: 24, of which 24 were waited for; matrix products, arithmetic and copies ran while one was open for 10% of the time, Pallas kernels for 0%

commit v1 on v0

v1 whole, which is shorter than its diff:
```python
import functools

import jax
import jax.numpy as jnp
from jax import lax
from jax.experimental import pallas as pl
from jax.experimental.pallas import tpu as pltpu
from jax.sharding import PartitionSpec as P

DEG = 8
MESH = pl.DeviceIdType.MESH
BF = jnp.bfloat16
F32 = jnp.float32


def build_kernel(slots, panel_cols, tile, rows_ref, cols_ref, live_ref, tiles_ref, out_ref, head, link, acc):
    block_row = pl.program_id(0)

    @pl.when(block_row == 0)
    def _():
        @pl.loop(0, pl.num_programs(0) * panel_cols)
        def _(b):
            head[b] = -1

        @pl.loop(0, slots)
        def _(s):
            @pl.when(live_ref[s] > 0)
            def _():
                b = rows_ref[s] * panel_cols + cols_ref[s]
                link[s] = head[b]
                head[b] = s

    for pair in range(panel_cols // 2):
        for side in range(2):
            s = head[block_row * panel_cols + 2 * pair + side]

            @pl.when(s < 0)
            def _(side=side):
                acc[side] = jnp.zeros((tile, tile), F32)

            @pl.when(s >= 0)
            def _(side=side, s=s):
                acc[side] = tiles_ref[s].astype(F32)

                def more(t):
                    acc[side] += tiles_ref[t].astype(F32)
                    return link[t]

                lax.while_loop(lambda t: t >= 0, more, link[s])

        both = jnp.concatenate([acc[0], acc[1]], axis=1)
        out_ref[:, pair * 2 * tile : (pair + 1) * 2 * tile] = both.astype(BF)


def build_panel(tiles, row_ids, col_ids, live, panel_rows, panel_cols):
    slots, tile, _ = tiles.shape
    smem = pl.BlockSpec(memory_space=pltpu.SMEM)
    return pl.pallas_call(
        functools.partial(build_kernel, slots, panel_cols, tile),
        grid=(panel_rows,),
        out_shape=jax.ShapeDtypeStruct((panel_rows * tile, panel_cols * tile), BF),
        in_specs=[smem, smem, smem, pl.BlockSpec((slots, tile, tile), lambda i: (0, 0, 0))],
        out_specs=pl.BlockSpec((tile, panel_cols * tile), lambda i: (i, 0)),
        scratch_shapes=[
            pltpu.SMEM((panel_rows * panel_cols,), jnp.int32),
            pltpu.SMEM((slots,), jnp.int32),
            pltpu.VMEM((2, tile, tile), F32),
        ],
        compiler_params=pltpu.CompilerParams(vmem_limit_bytes=32 * 2**20),
    )(row_ids, col_ids, live, tiles)


def filter_kernel(
    R, C, panel_ref, start_ref, center_ref, half_ref, out_ref, prev_ref,
    rowp, colp, sendr, sendc, redr, redc, mir, own,
    ps_row, ps_col, pr_row, pr_col, rs_row, rs_col, rr_row, rr_col,
):
    w = start_ref.shape[1]
    w2 = 2 * w
    Z = C // 2
    r = lax.axis_index("row")
    c = lax.axis_index("col")
    z, core = c // 2, c % 2
    root_row = c * R // C
    off = c * R % C
    is_root = r == root_row
    not_root = r != root_row
    col_home = (r * C + c) // R
    col_slot = c % R

    def col_of(d):
        return (c + d) % C

    def row_of(d):
        return (r + d) % R

    def chunk(d):
        return 2 * ((z // 2 + d // 2) % (Z // 2)) + (z % 2 + d % 2) % 2

    def remote(src, dst, send_sem, recv_sem, row, col):
        return pltpu.make_async_remote_copy(
            src_ref=src, dst_ref=dst, send_sem=send_sem, recv_sem=recv_sem,
            device_id=(row, col), device_id_type=MESH,
        )

    barrier = pltpu.get_barrier_semaphore()
    for d in range(1, C):
        pl.semaphore_signal(barrier, inc=1, device_id=(r, col_of(d)), device_id_type=MESH)
    for d in range(1, R):
        pl.semaphore_signal(barrier, inc=1, device_id=(row_of(d), col_home), device_id_type=MESH)

    @pl.when(not_root)
    def _():
        for i in range(R):
            pl.semaphore_signal(barrier, inc=1, device_id=(root_row, off + i), device_id_type=MESH)

    pl.semaphore_wait(barrier, jnp.where(is_root, C + R - 2, C + 2 * R - 2))

    out_ref[...] = start_ref[...]
    prev_ref[...] = start_ref[...]

    def p_row(par, d):
        return remote(rowp.at[par, c], rowp.at[par, c], ps_row.at[d], pr_row.at[par, c], r, col_of(d))

    def p_row_in(par, src):
        return remote(rowp.at[par, src], rowp.at[par, src], ps_row.at[0], pr_row.at[par, src], r, src)

    def p_col(par, d):
        return remote(rowp.at[par, c], colp.at[par, col_slot], ps_col.at[d], pr_col.at[par, col_slot], row_of(d), col_home)

    def p_col_in(par, i):
        return remote(colp.at[par, i], colp.at[par, i], ps_col.at[0], pr_col.at[par, i], root_row, off + i)

    def s_row(par, dst):
        return remote(sendr.at[dst], redr.at[par, c], rs_row.at[dst], rr_row.at[par, c], r, dst)

    def s_row_in(par, src):
        return remote(redr.at[par, src], redr.at[par, src], rs_row.at[src], rr_row.at[par, src], r, src)

    def s_col(par, i):
        return remote(sendc.at[i], redc.at[par, r], rs_col.at[i], rr_col.at[par, r], root_row, off + i)

    def s_col_in(par, src):
        return remote(redc.at[par, src], redc.at[par, src], rs_col.at[0], rr_col.at[par, src], src, col_home)

    def wait_sums_sent(par):
        for d in range(1, C):
            s_row(par, col_of(d)).wait_send()

        @pl.when(not_root)
        def _():
            for i in range(R):
                s_col(par, i).wait_send()

    def step(k, carry):
        par = k % 2
        rowp[par, c] = out_ref[...].astype(BF)
        for d in range(1, R):
            p_col(par, d).start()
        for d in range(C - 1, 0, -1):
            p_row(par, d).start()

        @pl.when(k > 0)
        def _():
            wait_sums_sent(1 - par)

        for d in range(Z):
            zz = chunk(d)
            if d == 0:
                p_row_in(par, c + 1 - 2 * core).wait_recv()
            else:
                p_row_in(par, 2 * zz).wait_recv()
                p_row_in(par, 2 * zz + 1).wait_recv()
            lhs = jnp.concatenate([rowp[par, 2 * zz], rowp[par, 2 * zz + 1]], axis=1)
            part = jnp.dot(lhs, panel_ref[pl.ds(zz * w2, w2), :], preferred_element_type=F32)
            for i in range(R // 2):
                piece = part[:, i * w2 : (i + 1) * w2]
                if d == 0:
                    mir[i] = piece
                else:
                    mir[i] += piece

        @pl.when(not_root)
        def _():
            for i in range(R):
                sendc[i] = mir[i // 2, :, (i % 2) * w : (i % 2 + 1) * w].astype(BF)
                s_col(par, i).start()
            for i in range(R):
                p_col_in(par, i).wait_recv()

        @pl.when(is_root)
        def _():
            for i in range(R):
                colp[par, i] = rowp[par, off + i]

        x_col = jnp.concatenate([colp[par, i] for i in range(R)], axis=1)
        for d in range(Z - 1, -1, -1):
            zz = chunk(d)
            part = lax.dot_general(
                x_col, panel_ref[pl.ds(zz * w2, w2), :], (((1,), (1,)), ((), ())),
                preferred_element_type=F32,
            )
            place = zz - off // 2
            inside = is_root & (place >= 0) & (place < R // 2)
            part = part + jnp.where(inside, mir[jnp.clip(place, 0, R // 2 - 1)], 0.0)
            left, right = part[:, :w], part[:, w:]
            sendr[2 * zz] = left.astype(BF)
            sendr[2 * zz + 1] = right.astype(BF)
            if d == 0:
                s_row(par, c + 1 - 2 * core).start()
                own[...] = jnp.where(core == 0, left, right)
            else:
                s_row(par, 2 * zz).start()
                s_row(par, 2 * zz + 1).start()

        total = own[...]
        for d in range(1, R):
            s_col_in(par, row_of(d)).wait_recv()
            total = total + redc[par, row_of(d)].astype(F32)
        for d in range(1, C):
            s_row_in(par, col_of(d)).wait_recv()
            total = total + redr[par, col_of(d)].astype(F32)

        first = k == 0
        scale = jnp.where(first, 1.0, 2.0)
        keep = jnp.where(first, 0.0, 1.0)
        current = out_ref[...]
        following = scale * (total - center_ref[0] * current) / half_ref[0] - keep * prev_ref[...]
        prev_ref[...] = current
        out_ref[...] = following
        for d in range(1, R):
            p_col(par, d).wait_send()
        for d in range(1, C):
            p_row(par, d).wait_send()
        return carry

    lax.fori_loop(0, DEG, step, 0)
    wait_sums_sent((DEG - 1) % 2)


def body(R, C, start_block, center, half_width, matrix_tiles, tile_row, tile_col, tile_live):
    vectors, w = start_block.shape
    tile = matrix_tiles.shape[-1]
    own_clusters = w // tile
    panel = build_panel(
        matrix_tiles[0], tile_row[0], tile_col[0], tile_live[0], own_clusters * C, own_clusters * R
    )
    vmem = pl.BlockSpec(memory_space=pltpu.VMEM)
    smem = pl.BlockSpec(memory_space=pltpu.SMEM)
    dma = pltpu.SemaphoreType.DMA
    flat = jax.ShapeDtypeStruct((vectors, w), F32)
    panel_bytes = panel.shape[0] * panel.shape[1] * 2
    return pl.pallas_call(
        functools.partial(filter_kernel, R, C),
        out_shape=(flat, flat),
        in_specs=[vmem, vmem, smem, smem],
        out_specs=(vmem, vmem),
        scratch_shapes=[
            pltpu.VMEM((2, C, vectors, w), BF),
            pltpu.VMEM((2, R, vectors, w), BF),
            pltpu.VMEM((C, vectors, w), BF),
            pltpu.VMEM((R, vectors, w), BF),
            pltpu.VMEM((2, C, vectors, w), BF),
            pltpu.VMEM((2, R, vectors, w), BF),
            pltpu.VMEM((R // 2, vectors, 2 * w), F32),
            pltpu.VMEM((vectors, w), F32),
            dma((C,)), dma((R,)), dma((2, C)), dma((2, R)),
            dma((C,)), dma((R,)), dma((2, C)), dma((2, R)),
        ],
        compiler_params=pltpu.CompilerParams(
            collective_id=0, has_side_effects=True, vmem_limit_bytes=panel_bytes + 14 * 2**20
        ),
    )(panel, start_block, center, half_width)


def solution(mesh):
    R, C = mesh.shape["row"], mesh.shape["col"]
    in_specs = (
        P(None, ("row", "col")),
        P(),
        P(),
        P("row", "col", None, None),
        P("row", "col"),
        P("row", "col"),
        P("row", "col"),
    )
    out_specs = (P(None, ("row", "col")), P(None, ("row", "col")))
    return jax.shard_map(
        functools.partial(body, R, C), mesh=mesh, in_specs=in_specs, out_specs=out_specs, check_vma=False
    )
```

time: 1120 us -> 168 us (0.15)
  waiting for transfers between devices: 832 us -> 0 us
  Pallas kernels: 0 us -> 159 us
  blocking collectives: 114 us -> 0 us
  matrix products: 90.7 us -> 0 us
  local copies, waits for them, and re-layouts: 30.8 us -> 5.54 us
  other arithmetic: 22.2 us -> 0 us
  between operations: 16.6 us -> 1.96 us
    psum x16 -> x0, waiting for transfers between devices: 578 us -> none  [the longest x8 310 us: body(): mirror_total = lax.psum(mirror_part, 'row')]
    reduce_scatter x8 -> x0, waiting for transfers between devices: 254 us -> none  [body(): lax.psum_scatter(partial_sum, 'col', scatter_dimension=1, tiled=True)]
    pallas_call x0 -> x2, Pallas kernels: none -> 159 us  [the longest x1 148 us: body(): pl.pallas_call(functools.partial(filter_kernel, R, C), out_shape=(flat, f...]
    all_gather x8 -> x0, blocking collectives: 114 us -> none  [body(): lax.all_gather(current.astype(jnp.bfloat16), 'col', axis=1, tiled=True)]
    dot_general x32 -> x0, matrix products: 90.7 us -> none  [the longest x8 31 us: body(): jnp.einsum('ksb,sab->ksa', x_col, stored, preferred_element_type=jnp.floa...]
    gather x16 -> x0, local copies, waits for them, and re-layouts: 17.1 us -> none  [the longest x8 12.1 us: body(): x_col = jnp.take(col_panel, col_ids, axis=1)]
    add x16 -> x0, local copies, waits for them, and re-layouts: 11.2 us -> none  [body(): partial_sum = row_part + placed]
  transfers between devices with their start and end apart: 24 -> 0, of which waited for: 24 -> 0; matrix products, arithmetic and copies ran while one was open for 10% -> 0% of each run, Pallas kernels for 0% -> 0%
where the time goes in v1:
time: 168 us; the launch traced here: 167 us
  Pallas kernels  159 us (95%)
  local copies, waits for them, and re-layouts  5.54 us (3%)
  between operations  1.96 us (1%)
    pallas_call x1, Pallas kernels, body(): pl.pallas_call(functools.partial(filter_kernel, R, C), out_shape=(flat, f...  148 us
    pallas_call x1, Pallas kernels, build_panel(): pl.pallas_call(functools.partial(build_kernel, slots, panel_cols, tile),...  11.3 us
    unnamed x12, local copies, waits for them, and re-layouts  5.54 us

profile of v1, /device:TPU:6, one launch (start us, length us, event | category | flops | bytes accessed | tf_op | source)
XLA Modules:
  0.0 166.9 jit_solution(12652206867997373014)
XLA Ops:
  1.9 0.0 copy-start
  1.9 2.3 %copy-done = bf16[1,48,192,192]{3,2,1,0:T(8,128)(2,1)S(1)} copy-done((bf16[1,48,192,192]{3,2,1,0:T(8,128)(2,1)S(1)}, bf16[1,48,192,192]{3,2,1,0:T(8,128)(2,1)}, u32[]{:S(2)}) %copy-start) | copy-done | bytes 3538968
  4.3 0.0 copy-start.2
  4.3 0.7 copy-done.2
  4.9 0.0 copy-start.3
  4.9 0.7 copy-done.3
  5.6 0.0 copy-start.4
  5.6 0.7 copy-done.4
  6.2 0.0 copy-start.1
  6.2 11.3 %shard_map.86.panel_ref = bf16[3072,1536]{1,0:T(8,128)(2,1)S(1)} custom-call(s32[48]{0:T(128)S(1)} %bitcast.5, s32[48]{0:T(128)S(1)} %bitcast.6, s32[48]{0:T(128)S(1)} %bitcast.7, bf16[48,192,192]{2,1,0:T(8,128)(2,1)S(1)} %bitcast.4), custom_call_target="tpu_custom_call" | custom-call | tf_op jit(solution)/shard_map/pallas_call | solution.py:58
  17.5 0.0 copy-done.1
  17.5 148.1 %shard_map.87 = (f32[32,384]{1,0:T(8,128)S(1)}, f32[32,384]{1,0:T(8,128)S(1)}) custom-call(bf16[3072,1536]{1,0:T(8,128)(2,1)S(1)} %shard_map.86.panel_ref, f32[32,384]{1,0:T(8,128)S(1)} %copy-done.1, f32[1]{0:T(128)S(6)} %copy.11.center_ref, f32[1]{0:T(128)S(6)} %copy.12.half_ref), custom_call_target="tpu_custom_call" | custom-call | tf_op jit(solution)/shard_map/pallas_call | solution.py:253
  165.7 0.6 copy.13
  166.3 0.6 copy.14
Async XLA Ops:
  1.9 2.3 %copy-start = (bf16[1,48,192,192]{3,2,1,0:T(8,128)(2,1)S(1)}, bf16[1,48,192,192]{3,2,1,0:T(8,128)(2,1)}, u32[]{:S(2)}) copy-start(bf16[1,48,192,192]{3,2,1,0:T(8,128)(2,1)} %param.10) | copy-start | bytes 10616836
  4.3 0.7 copy-start.2
  4.9 0.7 copy-start.3
  5.6 0.7 copy-start.4
  6.2 11.3 %copy-start.1 = (f32[32,384]{1,0:T(8,128)S(1)}, f32[32,384]{1,0:T(8,128)}, u32[]{:S(2)}) copy-start(f32[32,384]{1,0:T(8,128)} %start_ref.1) | copy-start | bytes 147460

commit v2 on v1

--- a/solution.py
+++ b/solution.py
@@ -31,25 +31,34 @@
                 head[b] = s
 
     for pair in range(panel_cols // 2):
-        for side in range(2):
-            s = head[block_row * panel_cols + 2 * pair + side]
-
-            @pl.when(s < 0)
-            def _(side=side):
-                acc[side] = jnp.zeros((tile, tile), F32)
-
-            @pl.when(s >= 0)
-            def _(side=side, s=s):
-                acc[side] = tiles_ref[s].astype(F32)
-
-                def more(t):
-                    acc[side] += tiles_ref[t].astype(F32)
-                    return link[t]
-
-                lax.while_loop(lambda t: t >= 0, more, link[s])
-
-        both = jnp.concatenate([acc[0], acc[1]], axis=1)
-        out_ref[:, pair * 2 * tile : (pair + 1) * 2 * tile] = both.astype(BF)
+        here = [head[block_row * panel_cols + 2 * pair + side] for side in range(2)]
+        empty = (here[0] < 0) & (here[1] < 0)
+        columns = slice(pair * 2 * tile, (pair + 1) * 2 * tile)
+
+        @pl.when(empty)
+        def _(columns=columns):
+            out_ref[:, columns] = jnp.zeros((tile, 2 * tile), BF)
+
+        @pl.when(jnp.logical_not(empty))
+        def _(columns=columns, here=here):
+            for side, s in enumerate(here):
+
+                @pl.when(s < 0)
+                def _(side=side):
+                    acc[side] = jnp.zeros((tile, tile), F32)
+
+                @pl.when(s >= 0)
+                def _(side=side, s=s):
+                    acc[side] = tiles_ref[s].astype(F32)
+
+                    def more(t):
+                        acc[side] += tiles_ref[t].astype(F32)
+                        return link[t]
+
+                    lax.while_loop(lambda t: t >= 0, more, link[s])
+
+            both = jnp.concatenate([acc[0], acc[1]], axis=1)
+            out_ref[:, columns] = both.astype(BF)
 
 
 def build_panel(tiles, row_ids, col_ids, live, panel_rows, panel_cols):
@@ -72,8 +81,8 @@
 
 def filter_kernel(
     R, C, panel_ref, start_ref, center_ref, half_ref, out_ref, prev_ref,
-    rowp, colp, sendr, sendc, redr, redc, mir, own,
-    ps_row, ps_col, pr_row, pr_col, rs_row, rs_col, rr_row, rr_col,
+    rowp, colp, sendr, sendc, sends, redr, redc, reds, mir, mine,
+    ps_row, ps_sib, ps_col, pr_row, pr_col, rs_row, rs_sib, rs_col, rr_row, rr_sib, rr_col,
 ):
     w = start_ref.shape[1]
     w2 = 2 * w
@@ -81,6 +90,7 @@
     r = lax.axis_index("row")
     c = lax.axis_index("col")
     z, core = c // 2, c % 2
+    sib = c + 1 - 2 * core
     root_row = c * R // C
     off = c * R % C
     is_root = r == root_row
@@ -88,13 +98,10 @@
     col_home = (r * C + c) // R
     col_slot = c % R
 
-    def col_of(d):
-        return (c + d) % C
-
     def row_of(d):
         return (r + d) % R
 
-    def chunk(d):
+    def chip(d):
         return 2 * ((z // 2 + d // 2) % (Z // 2)) + (z % 2 + d % 2) % 2
 
     def remote(src, dst, send_sem, recv_sem, row, col):
@@ -104,8 +111,9 @@
         )
 
     barrier = pltpu.get_barrier_semaphore()
-    for d in range(1, C):
-        pl.semaphore_signal(barrier, inc=1, device_id=(r, col_of(d)), device_id_type=MESH)
+    pl.semaphore_signal(barrier, inc=1, device_id=(r, sib), device_id_type=MESH)
+    for d in range(1, Z):
+        pl.semaphore_signal(barrier, inc=1, device_id=(r, 2 * chip(d) + core), device_id_type=MESH)
     for d in range(1, R):
         pl.semaphore_signal(barrier, inc=1, device_id=(row_of(d), col_home), device_id_type=MESH)
 
@@ -114,16 +122,20 @@
         for i in range(R):
             pl.semaphore_signal(barrier, inc=1, device_id=(root_row, off + i), device_id_type=MESH)
 
-    pl.semaphore_wait(barrier, jnp.where(is_root, C + R - 2, C + 2 * R - 2))
+    pl.semaphore_wait(barrier, jnp.where(is_root, Z + R - 1, Z + 2 * R - 1))
 
     out_ref[...] = start_ref[...]
     prev_ref[...] = start_ref[...]
 
     def p_row(par, d):
-        return remote(rowp.at[par, c], rowp.at[par, c], ps_row.at[d], pr_row.at[par, c], r, col_of(d))
-
-    def p_row_in(par, src):
+        return remote(rowp.at[par, c], rowp.at[par, c], ps_row.at[d], pr_row.at[par, c], r, 2 * chip(d) + core)
+
+    def p_in(par, src):
         return remote(rowp.at[par, src], rowp.at[par, src], ps_row.at[0], pr_row.at[par, src], r, src)
+
+    def p_sib(par, d):
+        src = 2 * chip(d) + core
+        return remote(rowp.at[par, src], rowp.at[par, src], ps_sib.at[d], pr_row.at[par, src], r, sib)
 
     def p_col(par, d):
         return remote(rowp.at[par, c], colp.at[par, col_slot], ps_col.at[d], pr_col.at[par, col_slot], row_of(d), col_home)
@@ -131,11 +143,16 @@
     def p_col_in(par, i):
         return remote(colp.at[par, i], colp.at[par, i], ps_col.at[0], pr_col.at[par, i], root_row, off + i)
 
-    def s_row(par, dst):
-        return remote(sendr.at[dst], redr.at[par, c], rs_row.at[dst], rr_row.at[par, c], r, dst)
-
-    def s_row_in(par, src):
-        return remote(redr.at[par, src], redr.at[par, src], rs_row.at[src], rr_row.at[par, src], r, src)
+    def s_row(par, d):
+        zz = chip(d)
+        return remote(sendr.at[zz], redr.at[par, z], rs_row.at[d], rr_row.at[par, z], r, 2 * zz + core)
+
+    def s_row_in(par, d):
+        zz = chip(d)
+        return remote(redr.at[par, zz], redr.at[par, zz], rs_row.at[0], rr_row.at[par, zz], r, 2 * zz + core)
+
+    def s_sib(par, d):
+        return remote(sends.at[d], reds.at[par, d], rs_sib.at[d], rr_sib.at[par, d], r, sib)
 
     def s_col(par, i):
         return remote(sendc.at[i], redc.at[par, r], rs_col.at[i], rr_col.at[par, r], root_row, off + i)
@@ -144,8 +161,10 @@
         return remote(redc.at[par, src], redc.at[par, src], rs_col.at[0], rr_col.at[par, src], src, col_home)
 
     def wait_sums_sent(par):
-        for d in range(1, C):
-            s_row(par, col_of(d)).wait_send()
+        for d in range(1, Z):
+            s_row(par, d).wait_send()
+        for d in range(Z):
+            s_sib(par, d).wait_send()
 
         @pl.when(not_root)
         def _():
@@ -155,22 +174,23 @@
     def step(k, carry):
         par = k % 2
         rowp[par, c] = out_ref[...].astype(BF)
+        p_sib(par, 0).start()
+        for d in range(Z - 1, 0, -1):
+            p_row(par, d).start()
         for d in range(1, R):
             p_col(par, d).start()
-        for d in range(C - 1, 0, -1):
-            p_row(par, d).start()
 
         @pl.when(k > 0)
         def _():
             wait_sums_sent(1 - par)
 
+        def arrive(d):
+            p_in(par, 2 * chip(d) + core).wait_recv()
+            p_sib(par, d).start()
+
         for d in range(Z):
-            zz = chunk(d)
-            if d == 0:
-                p_row_in(par, c + 1 - 2 * core).wait_recv()
-            else:
-                p_row_in(par, 2 * zz).wait_recv()
-                p_row_in(par, 2 * zz + 1).wait_recv()
+            zz = chip(d)
+            p_in(par, 2 * zz + 1 - core).wait_recv()
             lhs = jnp.concatenate([rowp[par, 2 * zz], rowp[par, 2 * zz + 1]], axis=1)
             part = jnp.dot(lhs, panel_ref[pl.ds(zz * w2, w2), :], preferred_element_type=F32)
             for i in range(R // 2):
@@ -179,6 +199,10 @@
                     mir[i] = piece
                 else:
                     mir[i] += piece
+            if d == 0:
+                arrive(1)
+            if d + 2 < Z:
+                arrive(d + 2)
 
         @pl.when(not_root)
         def _():
@@ -193,9 +217,14 @@
             for i in range(R):
                 colp[par, i] = rowp[par, off + i]
 
+        def pass_on(d):
+            s_sib(par, d).wait_recv()
+            sendr[chip(d)] = (mine[d] + reds[par, d]).astype(BF)
+            s_row(par, d).start()
+
         x_col = jnp.concatenate([colp[par, i] for i in range(R)], axis=1)
         for d in range(Z - 1, -1, -1):
-            zz = chunk(d)
+            zz = chip(d)
             part = lax.dot_general(
                 x_col, panel_ref[pl.ds(zz * w2, w2), :], (((1,), (1,)), ((), ())),
                 preferred_element_type=F32,
@@ -204,22 +233,20 @@
             inside = is_root & (place >= 0) & (place < R // 2)
             part = part + jnp.where(inside, mir[jnp.clip(place, 0, R // 2 - 1)], 0.0)
             left, right = part[:, :w], part[:, w:]
-            sendr[2 * zz] = left.astype(BF)
-            sendr[2 * zz + 1] = right.astype(BF)
-            if d == 0:
-                s_row(par, c + 1 - 2 * core).start()
-                own[...] = jnp.where(core == 0, left, right)
-            else:
-                s_row(par, 2 * zz).start()
-                s_row(par, 2 * zz + 1).start()
-
-        total = own[...]
+            sends[d] = jnp.where(core == 0, right, left)
+            s_sib(par, d).start()
+            mine[d] = jnp.where(core == 0, left, right)
+            if d + 1 < Z:
+                pass_on(d + 1)
+
+        s_sib(par, 0).wait_recv()
+        total = mine[0] + reds[par, 0]
         for d in range(1, R):
             s_col_in(par, row_of(d)).wait_recv()
             total = total + redc[par, row_of(d)].astype(F32)
-        for d in range(1, C):
-            s_row_in(par, col_of(d)).wait_recv()
-            total = total + redr[par, col_of(d)].astype(F32)
+        for d in range(1, Z):
+            s_row_in(par, d).wait_recv()
+            total = total + redr[par, chip(d)].astype(F32)
 
         first = k == 0
         scale = jnp.where(first, 1.0, 2.0)
@@ -230,8 +257,10 @@
         out_ref[...] = following
         for d in range(1, R):
             p_col(par, d).wait_send()
-        for d in range(1, C):
+        for d in range(1, Z):
             p_row(par, d).wait_send()
+        for d in range(Z):
+            p_sib(par, d).wait_send()
         return carry
 
     lax.fori_loop(0, DEG, step, 0)
@@ -249,6 +278,7 @@
     smem = pl.BlockSpec(memory_space=pltpu.SMEM)
     dma = pltpu.SemaphoreType.DMA
     flat = jax.ShapeDtypeStruct((vectors, w), F32)
+    Z = C // 2
     panel_bytes = panel.shape[0] * panel.shape[1] * 2
     return pl.pallas_call(
         functools.partial(filter_kernel, R, C),
@@ -258,14 +288,16 @@
         scratch_shapes=[
             pltpu.VMEM((2, C, vectors, w), BF),
             pltpu.VMEM((2, R, vectors, w), BF),
-            pltpu.VMEM((C, vectors, w), BF),
+            pltpu.VMEM((Z, vectors, w), BF),
             pltpu.VMEM((R, vectors, w), BF),
-            pltpu.VMEM((2, C, vectors, w), BF),
+            pltpu.VMEM((Z, vectors, w), F32),
+            pltpu.VMEM((2, Z, vectors, w), BF),
             pltpu.VMEM((2, R, vectors, w), BF),
+            pltpu.VMEM((2, Z, vectors, w), F32),
             pltpu.VMEM((R // 2, vectors, 2 * w), F32),
-            pltpu.VMEM((vectors, w), F32),
-            dma((C,)), dma((R,)), dma((2, C)), dma((2, R)),
-            dma((C,)), dma((R,)), dma((2, C)), dma((2, R)),
+            pltpu.VMEM((Z, vectors, w), F32),
+            dma((Z,)), dma((Z,)), dma((R,)), dma((2, C)), dma((2, R)),
+            dma((Z,)), dma((Z,)), dma((R,)), dma((2, Z)), dma((2, Z)), dma((2, R)),
         ],
         compiler_params=pltpu.CompilerParams(
             collective_id=0, has_side_effects=True, vmem_limit_bytes=panel_bytes + 14 * 2**20

time: 168 us -> 144 us (0.86)
  Pallas kernels: 159 us -> 135 us
    pallas_call x1, Pallas kernels: 148 us -> 130 us  [body(): pl.pallas_call(functools.partial(filter_kernel, R, C), out_shape=(flat, f...]
    pallas_call x1, Pallas kernels: 11.3 us -> 5.74 us  [build_panel(): pl.pallas_call(functools.partial(build_kernel, slots, panel_cols, tile),...]
where the time goes in v2:
time: 144 us; the launch traced here: 143 us
  Pallas kernels  135 us (94%)
  local copies, waits for them, and re-layouts  5.54 us (4%)
  between operations  1.96 us (1%)
    pallas_call x1, Pallas kernels, body(): pl.pallas_call(functools.partial(filter_kernel, R, C), out_shape=(flat, f...  130 us
    pallas_call x1, Pallas kernels, build_panel(): pl.pallas_call(functools.partial(build_kernel, slots, panel_cols, tile),...  5.74 us
    unnamed x12, local copies, waits for them, and re-layouts  5.54 us

profile of v2, /device:TPU:6, one launch (start us, length us, event | category | flops | bytes accessed | tf_op | source)
XLA Modules:
  0.0 143.0 jit_solution(1508481089859586185)
XLA Ops:
  1.9 0.0 copy-start
  1.9 2.3 %copy-done = bf16[1,48,192,192]{3,2,1,0:T(8,128)(2,1)S(1)} copy-done((bf16[1,48,192,192]{3,2,1,0:T(8,128)(2,1)S(1)}, bf16[1,48,192,192]{3,2,1,0:T(8,128)(2,1)}, u32[]{:S(2)}) %copy-start) | copy-done | bytes 3538968
  4.3 0.0 copy-start.2
  4.3 0.7 copy-done.2
  4.9 0.0 copy-start.3
  4.9 0.7 copy-done.3
  5.6 0.0 copy-start.4
  5.6 0.7 copy-done.4
  6.2 0.0 copy-start.1
  6.2 5.7 %shard_map.86.panel_ref = bf16[3072,1536]{1,0:T(8,128)(2,1)S(1)} custom-call(s32[48]{0:T(128)S(1)} %bitcast.5, s32[48]{0:T(128)S(1)} %bitcast.6, s32[48]{0:T(128)S(1)} %bitcast.7, bf16[48,192,192]{2,1,0:T(8,128)(2,1)S(1)} %bitcast.4), custom_call_target="tpu_custom_call" | custom-call | tf_op jit(solution)/shard_map/pallas_call | solution.py:67
  12.0 0.0 copy-done.1
  12.0 129.8 %shard_map.87 = (f32[32,384]{1,0:T(8,128)S(1)}, f32[32,384]{1,0:T(8,128)S(1)}) custom-call(bf16[3072,1536]{1,0:T(8,128)(2,1)S(1)} %shard_map.86.panel_ref, f32[32,384]{1,0:T(8,128)S(1)} %copy-done.1, f32[1]{0:T(128)S(6)} %copy.11.center_ref, f32[1]{0:T(128)S(6)} %copy.12.half_ref), custom_call_target="tpu_custom_call" | custom-call | tf_op jit(solution)/shard_map/pallas_call | solution.py:283
  141.8 0.6 copy.13
  142.4 0.6 copy.14
Async XLA Ops:
  1.9 2.3 %copy-start = (bf16[1,48,192,192]{3,2,1,0:T(8,128)(2,1)S(1)}, bf16[1,48,192,192]{3,2,1,0:T(8,128)(2,1)}, u32[]{:S(2)}) copy-start(bf16[1,48,192,192]{3,2,1,0:T(8,128)(2,1)} %param.10) | copy-start | bytes 10616836
  4.3 0.7 copy-start.2
  4.9 0.7 copy-start.3
  5.6 0.7 copy-start.4
  6.2 5.8 %copy-start.1 = (f32[32,384]{1,0:T(8,128)S(1)}, f32[32,384]{1,0:T(8,128)}, u32[]{:S(2)}) copy-start(f32[32,384]{1,0:T(8,128)} %start_ref.1) | copy-start | bytes 147460

commit v3 on v2

v3 whole, which is shorter than its diff:
```python
import functools

import jax
import jax.numpy as jnp
from jax import lax
from jax.experimental import pallas as pl
from jax.experimental.pallas import tpu as pltpu
from jax.sharding import PartitionSpec as P

DEG = 8
MESH = pl.DeviceIdType.MESH
BF = jnp.bfloat16
F32 = jnp.float32


def build_kernel(slots, panel_cols, tile, rows_ref, cols_ref, live_ref, tiles_ref, out_ref, head, link, acc):
    block_row = pl.program_id(0)

    @pl.when(block_row == 0)
    def _():
        @pl.loop(0, pl.num_programs(0) * panel_cols)
        def _(b):
            head[b] = -1

        @pl.loop(0, slots)
        def _(s):
            @pl.when(live_ref[s] > 0)
            def _():
                b = rows_ref[s] * panel_cols + cols_ref[s]
                link[s] = head[b]
                head[b] = s

    for pair in range(panel_cols // 2):
        here = [head[block_row * panel_cols + 2 * pair + side] for side in range(2)]
        empty = (here[0] < 0) & (here[1] < 0)
        columns = slice(pair * 2 * tile, (pair + 1) * 2 * tile)

        @pl.when(empty)
        def _(columns=columns):
            out_ref[:, columns] = jnp.zeros((tile, 2 * tile), BF)

        @pl.when(jnp.logical_not(empty))
        def _(columns=columns, here=here):
            for side, s in enumerate(here):

                @pl.when(s < 0)
                def _(side=side):
                    acc[side] = jnp.zeros((tile, tile), F32)

                @pl.when(s >= 0)
                def _(side=side, s=s):
                    acc[side] = tiles_ref[s].astype(F32)

                    def more(t):
                        acc[side] += tiles_ref[t].astype(F32)
                        return link[t]

                    lax.while_loop(lambda t: t >= 0, more, link[s])

            both = jnp.concatenate([acc[0], acc[1]], axis=1)
            out_ref[:, columns] = both.astype(BF)


def build_panel(tiles, row_ids, col_ids, live, panel_rows, panel_cols):
    slots, tile, _ = tiles.shape
    smem = pl.BlockSpec(memory_space=pltpu.SMEM)
    return pl.pallas_call(
        functools.partial(build_kernel, slots, panel_cols, tile),
        grid=(panel_rows,),
        out_shape=jax.ShapeDtypeStruct((panel_rows * tile, panel_cols * tile), BF),
        in_specs=[smem, smem, smem, pl.BlockSpec((slots, tile, tile), lambda i: (0, 0, 0))],
        out_specs=pl.BlockSpec((tile, panel_cols * tile), lambda i: (i, 0)),
        scratch_shapes=[
            pltpu.SMEM((panel_rows * panel_cols,), jnp.int32),
            pltpu.SMEM((slots,), jnp.int32),
            pltpu.VMEM((2, tile, tile), F32),
        ],
        compiler_params=pltpu.CompilerParams(vmem_limit_bytes=32 * 2**20),
    )(row_ids, col_ids, live, tiles)


def filter_kernel(
    R, C, panel_ref, start_ref, center_ref, half_ref, out_ref, prev_ref,
    cur, old, land, zbuf, colp, rowp, sends, reds, sendr, redr, sendc, redc, mir,
    ex_send, ex_recv, pz_send, pz_recv, pc_send, pc_recv, pl_send, ps_send, pr_recv,
    ss_send, ss_recv, sr_send, sr_recv, sc_send, sc_recv,
):
    w = start_ref.shape[1]
    w2 = 2 * w
    H = R // 2
    me = lax.axis_index("row")
    c = lax.axis_index("col")
    z, core = c // 2, c % 2
    sib = c + 1 - 2 * core
    is_hub = me == z
    not_hub = me != z

    flat_home = me * C + c
    to_row, to_col = flat_home % R, flat_home // R
    flat_own = c * R + me
    from_row, from_col = flat_own // C, flat_own % C
    moved = flat_home != flat_own
    stays = flat_home == flat_own

    def turn(i, d):
        return (i + d) % R

    def at(chip):
        return 2 * chip + core

    def remote(src, dst, send_sem, recv_sem, row, col):
        return pltpu.make_async_remote_copy(
            src_ref=src, dst_ref=dst, send_sem=send_sem, recv_sem=recv_sem,
            device_id=(row, col), device_id_type=MESH,
        )

    barrier = pltpu.get_barrier_semaphore()

    def greet(row, col):
        pl.semaphore_signal(barrier, inc=1, device_id=(row, col), device_id_type=MESH)

    greet(me, sib)
    for d in range(1, R):
        greet(me, at(turn(z, d)))
        greet(turn(me, d), c)

    @pl.when(not_hub)
    def _():
        for d in range(1, R):
            greet(z, at(turn(z, d)))

    @pl.when(moved)
    def _():
        greet(to_row, to_col)
        greet(from_row, from_col)

    pl.semaphore_wait(
        barrier, 2 * R - 1 + jnp.where(not_hub, R - 1, 0) + jnp.where(moved, 2, 0)
    )

    def enter():
        return remote(start_ref, cur, ex_send.at[0], ex_recv.at[0], to_row, to_col)

    def leave(i):
        src = cur if i == 0 else old
        return remote(src, land.at[i], ex_send.at[1 + i], ex_recv.at[1 + i], from_row, from_col)

    @pl.when(moved)
    def _():
        enter().start()
        enter().wait()

    @pl.when(stays)
    def _():
        cur[...] = start_ref[...]

    old[...] = jnp.zeros_like(old)

    def p_z(par, d):
        return remote(zbuf.at[par, z], zbuf.at[par, z], pz_send.at[d], pz_recv.at[par, z], me, at(turn(z, d)))

    def p_z_in(par, d):
        src = turn(z, d)
        return remote(zbuf.at[par, src], zbuf.at[par, src], pz_send.at[d], pz_recv.at[par, src], me, at(src))

    def p_col(par, d):
        return remote(zbuf.at[par, z], colp.at[par, me], pc_send.at[d], pc_recv.at[par, me], turn(me, d), c)

    def p_col_in(par, d):
        src = turn(me, d)
        return remote(colp.at[par, src], colp.at[par, src], pc_send.at[d], pc_recv.at[par, src], src, c)

    def p_relay(par, d):
        src = turn(z, d)
        return remote(zbuf.at[par, src], rowp.at[par, core, me], pl_send.at[d], pr_recv.at[par, core, me], src, c)

    def p_in(par, half, piece):
        ref = rowp.at[par, half, piece]
        return remote(ref, ref, pl_send.at[0], pr_recv.at[par, half, piece], me, sib)

    def p_sib(par, piece):
        ref = rowp.at[par, core, piece]
        return remote(ref, ref, ps_send.at[piece], pr_recv.at[par, core, piece], me, sib)

    def s_sib(par, j):
        return remote(sends.at[j], reds.at[par, j], ss_send.at[j], ss_recv.at[par, j], me, sib)

    def s_row(par, i):
        return remote(sendr.at[i], redr.at[par, z], sr_send.at[i], sr_recv.at[par, z], i, at(me))

    def s_row_in(par, i):
        return remote(redr.at[par, i], redr.at[par, i], sr_send.at[0], sr_recv.at[par, i], z, at(i))

    def s_col(par, d):
        return remote(sendc.at[d], redc.at[par, me], sc_send.at[d], sc_recv.at[par, me], turn(me, d), c)

    def s_col_in(par, d):
        src = turn(me, d)
        return remote(redc.at[par, src], redc.at[par, src], sc_send.at[d], sc_recv.at[par, src], src, c)

    def wait_sums_sent(par):
        for j in range(H):
            s_sib(par, j).wait_send()
        for i in range(R):

            @pl.when(not_hub | (me != i))
            def _(i=i):
                s_row(par, i).wait_send()

        for d in range(1, R):
            s_col(par, d).wait_send()

    def direct(x_col, half, j):
        rows = panel_ref[pl.ds((half * H + j) * w2, w2), :]
        return lax.dot_general(x_col, rows, (((1,), (1,)), ((), ())), preferred_element_type=F32)

    def mirrored(par, half, j):
        lhs = jnp.concatenate([rowp[par, half, 2 * j], rowp[par, half, 2 * j + 1]], axis=1)
        rows = panel_ref[pl.ds((half * H + j) * w2, w2), :]
        return jnp.dot(lhs, rows, preferred_element_type=F32)

    def step(k, carry):
        par = k % 2
        rounded = cur[...].astype(BF)
        zbuf[par, z] = rounded
        colp[par, me] = rounded
        for d in range(1, R):
            p_col(par, d).start()
        for d in range(1, R):
            p_z(par, d).start()

        @pl.when(k > 0)
        def _():
            wait_sums_sent(1 - par)

        for d in range(1, R):
            p_col_in(par, d).wait_recv()

        @pl.when(is_hub)
        def _():
            for i in range(R):
                rowp[par, core, i] = colp[par, i]
                p_sib(par, i).start()

        x_col = jnp.concatenate([colp[par, i] for i in range(R)], axis=1)
        for j in range(H):
            sends[j] = direct(x_col, 1 - core, j)
            s_sib(par, j).start()

        for d in range(1, R):
            p_z_in(par, d).wait_recv()

            @pl.when(turn(z, d) != me)
            def _(d=d):
                p_relay(par, d).start()

        @pl.when(not_hub)
        def _():
            rowp[par, core, me] = zbuf[par, me]
            p_sib(par, me).start()

        for j in range(H):
            part = direct(x_col, core, j)
            s_sib(par, j).wait_recv()
            part = part + reds[par, j]
            for i in range(2 * j, 2 * j + 2):
                piece = part[:, (i - 2 * j) * w : (i - 2 * j + 1) * w].astype(BF)
                sendr[i] = piece

                @pl.when(not_hub | (me != i))
                def _(i=i):
                    s_row(par, i).start()

                @pl.when(is_hub & (me == i))
                def _(piece=piece):
                    redr[par, z] = piece

            if j == 0:

                @pl.when(not_hub)
                def _():
                    for d in range(1, R):
                        p_in(par, core, turn(me, d)).wait_recv()
                        p_sib(par, turn(me, d)).start()

        total = mirrored(par, core, 0)
        for j in range(1, H):
            total = total + mirrored(par, core, j)
        for j in range(H):
            for i in range(2 * j, 2 * j + 2):
                p_in(par, 1 - core, i).wait_recv()
            total = total + mirrored(par, 1 - core, j)
        for i in range(R):
            mir[i] = total[:, i * w : (i + 1) * w]
        for d in range(1, R):
            sendc[d] = mir[turn(me, d)].astype(BF)
            s_col(par, d).start()

        product = mir[me]
        for i in range(R):

            @pl.when(not_hub | (me != i))
            def _(i=i):
                s_row_in(par, i).wait_recv()

            product = product + redr[par, i].astype(F32)
        for d in range(1, R):
            s_col_in(par, d).wait_recv()
            product = product + redc[par, turn(me, d)].astype(F32)

        first = k == 0
        scale = jnp.where(first, 1.0, 2.0)
        keep = jnp.where(first, 0.0, 1.0)
        current = cur[...]
        following = scale * (product - center_ref[0] * current) / half_ref[0] - keep * old[...]
        old[...] = current
        cur[...] = following
        for d in range(1, R):
            p_col(par, d).wait_send()
            p_z(par, d).wait_send()

            @pl.when(turn(z, d) != me)
            def _(d=d):
                p_relay(par, d).wait_send()

        for i in range(R):
            p_sib(par, i).wait_send()
        return carry

    lax.fori_loop(0, DEG, step, 0)
    wait_sums_sent((DEG - 1) % 2)

    @pl.when(moved)
    def _():
        for i in range(2):
            leave(i).start()
        for i in range(2):
            leave(i).wait()
        out_ref[...] = land[0]
        prev_ref[...] = land[1]

    @pl.when(stays)
    def _():
        out_ref[...] = cur[...]
        prev_ref[...] = old[...]


def body(R, C, start_block, center, half_width, matrix_tiles, tile_row, tile_col, tile_live):
    vectors, w = start_block.shape
    tile = matrix_tiles.shape[-1]
    own_clusters = w // tile
    panel = build_panel(
        matrix_tiles[0], tile_row[0], tile_col[0], tile_live[0], own_clusters * C, own_clusters * R
    )
    vmem = pl.BlockSpec(memory_space=pltpu.VMEM)
    smem = pl.BlockSpec(memory_space=pltpu.SMEM)
    dma = pltpu.SemaphoreType.DMA
    flat = jax.ShapeDtypeStruct((vectors, w), F32)
    panel_bytes = panel.shape[0] * panel.shape[1] * 2
    return pl.pallas_call(
        functools.partial(filter_kernel, R, C),
        out_shape=(flat, flat),
        in_specs=[vmem, vmem, smem, smem],
        out_specs=(vmem, vmem),
        scratch_shapes=[
            pltpu.VMEM((vectors, w), F32),
            pltpu.VMEM((vectors, w), F32),
            pltpu.VMEM((2, vectors, w), F32),
            pltpu.VMEM((2, R, vectors, w), BF),
            pltpu.VMEM((2, R, vectors, w), BF),
            pltpu.VMEM((2, 2, R, vectors, w), BF),
            pltpu.VMEM((R // 2, vectors, 2 * w), F32),
            pltpu.VMEM((2, R // 2, vectors, 2 * w), F32),
            pltpu.VMEM((R, vectors, w), BF),
            pltpu.VMEM((2, R, vectors, w), BF),
            pltpu.VMEM((R, vectors, w), BF),
            pltpu.VMEM((2, R, vectors, w), BF),
            pltpu.VMEM((R, vectors, w), F32),
            dma((3,)), dma((3,)),
            dma((R,)), dma((2, R)), dma((R,)), dma((2, R)), dma((R,)), dma((R,)), dma((2, 2, R)),
            dma((R // 2,)), dma((2, R // 2)), dma((R,)), dma((2, R)), dma((R,)), dma((2, R)),
        ],
        compiler_params=pltpu.CompilerParams(
            collective_id=0, has_side_effects=True, vmem_limit_bytes=panel_bytes + 14 * 2**20
        ),
    )(panel, start_block, center, half_width)


def solution(mesh):
    R, C = mesh.shape["row"], mesh.shape["col"]
    assert C == 2 * R and R % 2 == 0
    in_specs = (
        P(None, ("row", "col")),
        P(),
        P(),
        P("row", "col", None, None),
        P("row", "col"),
        P("row", "col"),
        P("row", "col"),
    )
    out_specs = (P(None, ("row", "col")), P(None, ("row", "col")))
    return jax.shard_map(
        functools.partial(body, R, C), mesh=mesh, in_specs=in_specs, out_specs=out_specs, check_vma=False
    )
```

time: 144 us -> 157 us (1.090)
  Pallas kernels: 135 us -> 149 us
    pallas_call x1, Pallas kernels: 130 us -> 144 us  [body(): pl.pallas_call(functools.partial(filter_kernel, R, C), out_shape=(flat, f...]
where the time goes in v3:
time: 157 us
  Pallas kernels  149 us (95%)
  local copies, waits for them, and re-layouts  5.54 us (4%)
  between operations  1.96 us (1%)
    pallas_call x1, Pallas kernels, body(): pl.pallas_call(functools.partial(filter_kernel, R, C), out_shape=(flat, f...  144 us
    pallas_call x1, Pallas kernels, build_panel(): pl.pallas_call(functools.partial(build_kernel, slots, panel_cols, tile),...  5.56 us
    unnamed x12, local copies, waits for them, and re-layouts  5.54 us

profile of v3, /device:TPU:6, one launch (start us, length us, event | category | flops | bytes accessed | tf_op | source)
XLA Modules:
  0.0 156.6 jit_solution(2256515343219463030)
XLA Ops:
  1.9 0.0 copy-start
  1.9 2.3 %copy-done = bf16[1,48,192,192]{3,2,1,0:T(8,128)(2,1)S(1)} copy-done((bf16[1,48,192,192]{3,2,1,0:T(8,128)(2,1)S(1)}, bf16[1,48,192,192]{3,2,1,0:T(8,128)(2,1)}, u32[]{:S(2)}) %copy-start) | copy-done | bytes 3538968
  4.3 0.0 copy-start.2
  4.3 0.7 copy-done.2
  4.9 0.0 copy-start.3
  4.9 0.7 copy-done.3
  5.6 0.0 copy-start.4
  5.6 0.7 copy-done.4
  6.2 0.0 copy-start.1
  6.2 5.6 %shard_map.86.panel_ref = bf16[3072,1536]{1,0:T(8,128)(2,1)S(1)} custom-call(s32[48]{0:T(128)S(1)} %bitcast.5, s32[48]{0:T(128)S(1)} %bitcast.6, s32[48]{0:T(128)S(1)} %bitcast.7, bf16[48,192,192]{2,1,0:T(8,128)(2,1)S(1)} %bitcast.4), custom_call_target="tpu_custom_call" | custom-call | tf_op jit(solution)/shard_map/pallas_call | solution.py:67
  11.8 0.0 copy-done.1
  11.8 143.6 %shard_map.87 = (f32[32,384]{1,0:T(8,128)S(1)}, f32[32,384]{1,0:T(8,128)S(1)}) custom-call(bf16[3072,1536]{1,0:T(8,128)(2,1)S(1)} %shard_map.86.panel_ref, f32[32,384]{1,0:T(8,128)S(1)} %copy-done.1, f32[1]{0:T(128)S(6)} %copy.11.center_ref, f32[1]{0:T(128)S(6)} %copy.12.half_ref), custom_call_target="tpu_custom_call" | custom-call | tf_op jit(solution)/shard_map/pallas_call | solution.py:360
  155.4 0.6 copy.13
  156.0 0.6 copy.14
Async XLA Ops:
  1.9 2.3 %copy-start = (bf16[1,48,192,192]{3,2,1,0:T(8,128)(2,1)S(1)}, bf16[1,48,192,192]{3,2,1,0:T(8,128)(2,1)}, u32[]{:S(2)}) copy-start(bf16[1,48,192,192]{3,2,1,0:T(8,128)(2,1)} %param.10) | copy-start | bytes 10616836
  4.3 0.7 copy-start.2
  4.9 0.7 copy-start.3
  5.6 0.7 copy-start.4
  6.2 5.6 %copy-start.1 = (f32[32,384]{1,0:T(8,128)S(1)}, f32[32,384]{1,0:T(8,128)}, u32[]{:S(2)}) copy-start(f32[32,384]{1,0:T(8,128)} %start_ref.1) | copy-start | bytes 147460

commit v4 on v2

--- a/solution.py
+++ b/solution.py
@@ -13,8 +13,12 @@
 F32 = jnp.float32
 
 
-def build_kernel(slots, panel_cols, tile, rows_ref, cols_ref, live_ref, tiles_ref, out_ref, head, link, acc):
+def build_kernel(slots, panel_cols, tile, flip, rows_ref, cols_ref, live_ref, tiles_ref, out_ref, head, link, acc):
     block_row = pl.program_id(0)
+
+    def load(s):
+        wide = tiles_ref[s].astype(F32)
+        return wide.T if flip else wide
 
     @pl.when(block_row == 0)
     def _():
@@ -49,10 +53,10 @@
 
                 @pl.when(s >= 0)
                 def _(side=side, s=s):
-                    acc[side] = tiles_ref[s].astype(F32)
+                    acc[side] = load(s)
 
                     def more(t):
-                        acc[side] += tiles_ref[t].astype(F32)
+                        acc[side] += load(t)
                         return link[t]
 
                     lax.while_loop(lambda t: t >= 0, more, link[s])
@@ -61,11 +65,11 @@
             out_ref[:, columns] = both.astype(BF)
 
 
-def build_panel(tiles, row_ids, col_ids, live, panel_rows, panel_cols):
+def build_panel(tiles, row_ids, col_ids, live, panel_rows, panel_cols, flip=False):
     slots, tile, _ = tiles.shape
     smem = pl.BlockSpec(memory_space=pltpu.SMEM)
     return pl.pallas_call(
-        functools.partial(build_kernel, slots, panel_cols, tile),
+        functools.partial(build_kernel, slots, panel_cols, tile, flip),
         grid=(panel_rows,),
         out_shape=jax.ShapeDtypeStruct((panel_rows * tile, panel_cols * tile), BF),
         in_specs=[smem, smem, smem, pl.BlockSpec((slots, tile, tile), lambda i: (0, 0, 0))],
@@ -80,7 +84,7 @@
 
 
 def filter_kernel(
-    R, C, panel_ref, start_ref, center_ref, half_ref, out_ref, prev_ref,
+    R, C, both, panel_ref, flipped_ref, start_ref, center_ref, half_ref, out_ref, prev_ref,
     rowp, colp, sendr, sendc, sends, redr, redc, reds, mir, mine,
     ps_row, ps_sib, ps_col, pr_row, pr_col, rs_row, rs_sib, rs_col, rr_row, rr_sib, rr_col,
 ):
@@ -225,10 +229,14 @@
         x_col = jnp.concatenate([colp[par, i] for i in range(R)], axis=1)
         for d in range(Z - 1, -1, -1):
             zz = chip(d)
-            part = lax.dot_general(
-                x_col, panel_ref[pl.ds(zz * w2, w2), :], (((1,), (1,)), ((), ())),
-                preferred_element_type=F32,
-            )
+            if both:
+                columns = pl.ds(pl.multiple_of(zz * w2, w2), w2)
+                part = jnp.dot(x_col, flipped_ref[:, columns], preferred_element_type=F32)
+            else:
+                part = lax.dot_general(
+                    x_col, panel_ref[pl.ds(zz * w2, w2), :], (((1,), (1,)), ((), ())),
+                    preferred_element_type=F32,
+                )
             place = zz - off // 2
             inside = is_root & (place >= 0) & (place < R // 2)
             part = part + jnp.where(inside, mir[jnp.clip(place, 0, R // 2 - 1)], 0.0)
@@ -271,19 +279,24 @@
     vectors, w = start_block.shape
     tile = matrix_tiles.shape[-1]
     own_clusters = w // tile
-    panel = build_panel(
-        matrix_tiles[0], tile_row[0], tile_col[0], tile_live[0], own_clusters * C, own_clusters * R
-    )
+    ids = (tile_row[0], tile_col[0])
+    sizes = (own_clusters * C, own_clusters * R)
+    panel = build_panel(matrix_tiles[0], *ids, tile_live[0], *sizes)
+    both = 2 * panel.size * 2 <= 24 * 2**20
+    if both:
+        flipped = build_panel(matrix_tiles[0], *ids[::-1], tile_live[0], *sizes[::-1], flip=True)
+    else:
+        flipped = jnp.zeros((16, 128), BF)
     vmem = pl.BlockSpec(memory_space=pltpu.VMEM)
     smem = pl.BlockSpec(memory_space=pltpu.SMEM)
     dma = pltpu.SemaphoreType.DMA
     flat = jax.ShapeDtypeStruct((vectors, w), F32)
     Z = C // 2
-    panel_bytes = panel.shape[0] * panel.shape[1] * 2
+    panel_bytes = (panel.size + flipped.size) * 2
     return pl.pallas_call(
-        functools.partial(filter_kernel, R, C),
+        functools.partial(filter_kernel, R, C, both),
         out_shape=(flat, flat),
-        in_specs=[vmem, vmem, smem, smem],
+        in_specs=[vmem, vmem, vmem, smem, smem],
         out_specs=(vmem, vmem),
         scratch_shapes=[
             pltpu.VMEM((2, C, vectors, w), BF),
@@ -302,7 +315,7 @@
         compiler_params=pltpu.CompilerParams(
             collective_id=0, has_side_effects=True, vmem_limit_bytes=panel_bytes + 14 * 2**20
         ),
-    )(panel, start_block, center, half_width)
+    )(panel, flipped, start_block, center, half_width)
 
 
 def solution(mesh):

time: 144 us -> 145 us (level)
    pallas_call x2 -> x3, Pallas kernels: 135 us -> 135 us  [the longest x1 122 us: body(): pl.pallas_call(functools.partial(filter_kernel, R, C, both), out_shape=(f...]
where the time goes in v4:
time: 145 us; the launch traced here: 143 us
  Pallas kernels  135 us (93%)
  local copies, waits for them, and re-layouts  5.54 us (4%)
  between operations  1.97 us (1%)
    pallas_call x1, Pallas kernels, body(): pl.pallas_call(functools.partial(filter_kernel, R, C, both), out_shape=(f...  122 us
    pallas_call x2, Pallas kernels, build_panel(): pl.pallas_call(functools.partial(build_kernel, slots, panel_cols, tile, f...  12.8 us
    unnamed x12, local copies, waits for them, and re-layouts  5.54 us

profile of v4, /device:TPU:6, one launch (start us, length us, event | category | flops | bytes accessed | tf_op | source)
XLA Modules:
  0.0 142.7 jit_solution(16343624919373987167)
XLA Ops:
  1.9 0.0 copy-start
  1.9 2.3 %copy-done = bf16[1,48,192,192]{3,2,1,0:T(8,128)(2,1)S(1)} copy-done((bf16[1,48,192,192]{3,2,1,0:T(8,128)(2,1)S(1)}, bf16[1,48,192,192]{3,2,1,0:T(8,128)(2,1)}, u32[]{:S(2)}) %copy-start) | copy-done | bytes 3538968
  4.3 0.0 copy-start.2
  4.3 0.7 copy-done.2
  4.9 0.0 copy-start.3
  4.9 0.7 copy-done.3
  5.6 0.0 copy-start.4
  5.6 0.7 copy-done.4
  6.2 7.5 %shard_map.87.flipped_ref = bf16[1536,3072]{1,0:T(8,128)(2,1)S(1)} custom-call(s32[48]{0:T(128)S(1)} %bitcast.8, s32[48]{0:T(128)S(1)} %bitcast.6, s32[48]{0:T(128)S(1)} %bitcast.10, bf16[48,192,192]{2,1,0:T(8,128)(2,1)S(1)} %bitcast.4), custom_call_target="tpu_custom_call" | custom-call | tf_op jit(solution)/shard_map/pallas_call | solution.py:71
  13.7 0.0 copy-start.1
  13.7 5.4 %shard_map.86.panel_ref = bf16[3072,1536]{1,0:T(8,128)(2,1)S(1)} custom-call(s32[48]{0:T(128)S(1)} %bitcast.7, s32[48]{0:T(128)S(1)} %bitcast.9, s32[48]{0:T(128)S(1)} %bitcast.11, bf16[48,192,192]{2,1,0:T(8,128)(2,1)S(1)} %bitcast.5), custom_call_target="tpu_custom_call" | custom-call | tf_op jit(solution)/shard_map/pallas_call | solution.py:71
  19.1 0.0 copy-done.1
  19.1 122.3 %shard_map.88 = (f32[32,384]{1,0:T(8,128)S(1)}, f32[32,384]{1,0:T(8,128)S(1)}) custom-call(bf16[3072,1536]{1,0:T(8,128)(2,1)S(1)} %shard_map.86.panel_ref, bf16[1536,3072]{1,0:T(8,128)(2,1)S(1)} %shard_map.87.flipped_ref, f32[32,384]{1,0:T(8,128)S(1)} %copy-done.1, f32[1]{0:T(128)S(6)} %copy.11.center_ref, f32[1]{0:T(128)S(6)} %copy.12.half_ref), custom_call_target="tpu_custom_call" | custom-call | tf_op jit(solution)/shard_map/pallas_call | solution.py:296
  141.5 0.6 copy.13
  142.1 0.6 copy.14
Async XLA Ops:
  1.9 2.3 %copy-start = (bf16[1,48,192,192]{3,2,1,0:T(8,128)(2,1)S(1)}, bf16[1,48,192,192]{3,2,1,0:T(8,128)(2,1)}, u32[]{:S(2)}) copy-start(bf16[1,48,192,192]{3,2,1,0:T(8,128)(2,1)} %param.10) | copy-start | bytes 10616836
  4.3 0.7 copy-start.2
  4.9 0.7 copy-start.3
  5.6 0.7 copy-start.4
  13.7 5.4 %copy-start.1 = (f32[32,384]{1,0:T(8,128)S(1)}, f32[32,384]{1,0:T(8,128)}, u32[]{:S(2)}) copy-start(f32[32,384]{1,0:T(8,128)} %start_ref.1) | copy-start | bytes 147460

commit v5 on v3

--- a/solution.py
+++ b/solution.py
@@ -13,8 +13,12 @@
 F32 = jnp.float32
 
 
-def build_kernel(slots, panel_cols, tile, rows_ref, cols_ref, live_ref, tiles_ref, out_ref, head, link, acc):
+def build_kernel(slots, panel_cols, tile, flip, rows_ref, cols_ref, live_ref, tiles_ref, out_ref, head, link, acc):
     block_row = pl.program_id(0)
+
+    def load(s):
+        wide = tiles_ref[s].astype(F32)
+        return wide.T if flip else wide
 
     @pl.when(block_row == 0)
     def _():
@@ -49,10 +53,10 @@
 
                 @pl.when(s >= 0)
                 def _(side=side, s=s):
-                    acc[side] = tiles_ref[s].astype(F32)
+                    acc[side] = load(s)
 
                     def more(t):
-                        acc[side] += tiles_ref[t].astype(F32)
+                        acc[side] += load(t)
                         return link[t]
 
                     lax.while_loop(lambda t: t >= 0, more, link[s])
@@ -61,11 +65,11 @@
             out_ref[:, columns] = both.astype(BF)
 
 
-def build_panel(tiles, row_ids, col_ids, live, panel_rows, panel_cols):
+def build_panel(tiles, row_ids, col_ids, live, panel_rows, panel_cols, flip=False):
     slots, tile, _ = tiles.shape
     smem = pl.BlockSpec(memory_space=pltpu.SMEM)
     return pl.pallas_call(
-        functools.partial(build_kernel, slots, panel_cols, tile),
+        functools.partial(build_kernel, slots, panel_cols, tile, flip),
         grid=(panel_rows,),
         out_shape=jax.ShapeDtypeStruct((panel_rows * tile, panel_cols * tile), BF),
         in_specs=[smem, smem, smem, pl.BlockSpec((slots, tile, tile), lambda i: (0, 0, 0))],
@@ -80,10 +84,10 @@
 
 
 def filter_kernel(
-    R, C, panel_ref, start_ref, center_ref, half_ref, out_ref, prev_ref,
-    cur, old, land, zbuf, colp, rowp, sends, reds, sendr, redr, sendc, redc, mir,
+    R, C, both, panel_ref, flipped_ref, start_ref, center_ref, half_ref, out_ref, prev_ref,
+    cur, old, land, zbuf, colp, rowp, sends, reds, sendr, rbuf, redr, sendc, redc, mir,
     ex_send, ex_recv, pz_send, pz_recv, pc_send, pc_recv, pl_send, ps_send, pr_recv,
-    ss_send, ss_recv, sr_send, sr_recv, sc_send, sc_recv,
+    ss_send, ss_recv, sx_send, sx_recv, sr_send, sr_recv, sc_send, sc_recv,
 ):
     w = start_ref.shape[1]
     w2 = 2 * w
@@ -124,19 +128,12 @@
         greet(me, at(turn(z, d)))
         greet(turn(me, d), c)
 
-    @pl.when(not_hub)
-    def _():
-        for d in range(1, R):
-            greet(z, at(turn(z, d)))
-
     @pl.when(moved)
     def _():
         greet(to_row, to_col)
         greet(from_row, from_col)
 
-    pl.semaphore_wait(
-        barrier, 2 * R - 1 + jnp.where(not_hub, R - 1, 0) + jnp.where(moved, 2, 0)
-    )
+    pl.semaphore_wait(barrier, 2 * R - 1 + jnp.where(moved, 2, 0))
 
     def enter():
         return remote(start_ref, cur, ex_send.at[0], ex_recv.at[0], to_row, to_col)
@@ -185,11 +182,20 @@
     def s_sib(par, j):
         return remote(sends.at[j], reds.at[par, j], ss_send.at[j], ss_recv.at[par, j], me, sib)
 
-    def s_row(par, i):
-        return remote(sendr.at[i], redr.at[par, z], sr_send.at[i], sr_recv.at[par, z], i, at(me))
-
-    def s_row_in(par, i):
-        return remote(redr.at[par, i], redr.at[par, i], sr_send.at[0], sr_recv.at[par, i], z, at(i))
+    def s_plane(par, d):
+        dst = turn(me, d)
+        return remote(sendr.at[dst], rbuf.at[par, me], sx_send.at[d], sx_recv.at[par, me], dst, c)
+
+    def s_plane_in(par, src):
+        return remote(rbuf.at[par, src], rbuf.at[par, src], sx_send.at[0], sx_recv.at[par, src], src, c)
+
+    def s_row(par, d):
+        dst = turn(z, d)
+        return remote(rbuf.at[par, dst], redr.at[par, z], sr_send.at[d], sr_recv.at[par, z], me, at(dst))
+
+    def s_row_in(par, d):
+        src = turn(z, d)
+        return remote(redr.at[par, src], redr.at[par, src], sr_send.at[d], sr_recv.at[par, src], me, at(src))
 
     def s_col(par, d):
         return remote(sendc.at[d], redc.at[par, me], sc_send.at[d], sc_recv.at[par, me], turn(me, d), c)
@@ -201,17 +207,16 @@
     def wait_sums_sent(par):
         for j in range(H):
             s_sib(par, j).wait_send()
-        for i in range(R):
-
-            @pl.when(not_hub | (me != i))
-            def _(i=i):
-                s_row(par, i).wait_send()
-
-        for d in range(1, R):
+        for d in range(1, R):
+            s_plane(par, d).wait_send()
+            s_row(par, d).wait_send()
             s_col(par, d).wait_send()
 
     def direct(x_col, half, j):
-        rows = panel_ref[pl.ds((half * H + j) * w2, w2), :]
+        place = pl.ds(pl.multiple_of((half * H + j) * w2, w2), w2)
+        if both:
+            return jnp.dot(x_col, flipped_ref[:, place], preferred_element_type=F32)
+        rows = panel_ref[place, :]
         return lax.dot_general(x_col, rows, (((1,), (1,)), ((), ())), preferred_element_type=F32)
 
     def mirrored(par, half, j):
@@ -264,17 +269,7 @@
             s_sib(par, j).wait_recv()
             part = part + reds[par, j]
             for i in range(2 * j, 2 * j + 2):
-                piece = part[:, (i - 2 * j) * w : (i - 2 * j + 1) * w].astype(BF)
-                sendr[i] = piece
-
-                @pl.when(not_hub | (me != i))
-                def _(i=i):
-                    s_row(par, i).start()
-
-                @pl.when(is_hub & (me == i))
-                def _(piece=piece):
-                    redr[par, z] = piece
-
+                sendr[i] = part[:, (i - 2 * j) * w : (i - 2 * j + 1) * w].astype(BF)
             if j == 0:
 
                 @pl.when(not_hub)
@@ -283,9 +278,22 @@
                         p_in(par, core, turn(me, d)).wait_recv()
                         p_sib(par, turn(me, d)).start()
 
+        rbuf[par, me] = sendr[me]
+        for d in range(1, R):
+            s_plane(par, d).start()
+
         total = mirrored(par, core, 0)
         for j in range(1, H):
             total = total + mirrored(par, core, j)
+
+        for d in range(1, R):
+
+            @pl.when(turn(z, d) != me)
+            def _(d=d):
+                s_plane_in(par, turn(z, d)).wait_recv()
+
+            s_row(par, d).start()
+
         for j in range(H):
             for i in range(2 * j, 2 * j + 2):
                 p_in(par, 1 - core, i).wait_recv()
@@ -296,14 +304,14 @@
             sendc[d] = mir[turn(me, d)].astype(BF)
             s_col(par, d).start()
 
-        product = mir[me]
-        for i in range(R):
-
-            @pl.when(not_hub | (me != i))
-            def _(i=i):
-                s_row_in(par, i).wait_recv()
-
-            product = product + redr[par, i].astype(F32)
+        @pl.when(not_hub)
+        def _():
+            s_plane_in(par, z).wait_recv()
+
+        product = mir[me] + rbuf[par, z].astype(F32)
+        for d in range(1, R):
+            s_row_in(par, d).wait_recv()
+            product = product + redr[par, turn(z, d)].astype(F32)
         for d in range(1, R):
             s_col_in(par, d).wait_recv()
             product = product + redc[par, turn(me, d)].astype(F32)
@@ -349,18 +357,23 @@
     vectors, w = start_block.shape
     tile = matrix_tiles.shape[-1]
     own_clusters = w // tile
-    panel = build_panel(
-        matrix_tiles[0], tile_row[0], tile_col[0], tile_live[0], own_clusters * C, own_clusters * R
-    )
+    ids = (tile_row[0], tile_col[0])
+    sizes = (own_clusters * C, own_clusters * R)
+    panel = build_panel(matrix_tiles[0], *ids, tile_live[0], *sizes)
+    both = 2 * panel.size * 2 <= 24 * 2**20
+    if both:
+        flipped = build_panel(matrix_tiles[0], *ids[::-1], tile_live[0], *sizes[::-1], flip=True)
+    else:
+        flipped = jnp.zeros((16, 128), BF)
     vmem = pl.BlockSpec(memory_space=pltpu.VMEM)
     smem = pl.BlockSpec(memory_space=pltpu.SMEM)
     dma = pltpu.SemaphoreType.DMA
     flat = jax.ShapeDtypeStruct((vectors, w), F32)
-    panel_bytes = panel.shape[0] * panel.shape[1] * 2
+    panel_bytes = (panel.size + flipped.size) * 2
     return pl.pallas_call(
-        functools.partial(filter_kernel, R, C),
+        functools.partial(filter_kernel, R, C, both),
         out_shape=(flat, flat),
-        in_specs=[vmem, vmem, smem, smem],
+        in_specs=[vmem, vmem, vmem, smem, smem],
         out_specs=(vmem, vmem),
         scratch_shapes=[
             pltpu.VMEM((vectors, w), F32),
@@ -373,17 +386,18 @@
             pltpu.VMEM((2, R // 2, vectors, 2 * w), F32),
             pltpu.VMEM((R, vectors, w), BF),
             pltpu.VMEM((2, R, vectors, w), BF),
+            pltpu.VMEM((2, R, vectors, w), BF),
             pltpu.VMEM((R, vectors, w), BF),
             pltpu.VMEM((2, R, vectors, w), BF),
             pltpu.VMEM((R, vectors, w), F32),
             dma((3,)), dma((3,)),
             dma((R,)), dma((2, R)), dma((R,)), dma((2, R)), dma((R,)), dma((R,)), dma((2, 2, R)),
-            dma((R // 2,)), dma((2, R // 2)), dma((R,)), dma((2, R)), dma((R,)), dma((2, R)),
+            dma((R // 2,)), dma((2, R // 2)), dma((R,)), dma((2, R)), dma((R,)), dma((2, R)), dma((R,)), dma((2, R)),
         ],
         compiler_params=pltpu.CompilerParams(
             collective_id=0, has_side_effects=True, vmem_limit_bytes=panel_bytes + 14 * 2**20
         ),
-    )(panel, start_block, center, half_width)
+    )(panel, flipped, start_block, center, half_width)
 
 
 def solution(mesh):

time: 157 us -> 174 us (1.11)
  Pallas kernels: 149 us -> 167 us
    pallas_call x2 -> x3, Pallas kernels: 149 us -> 167 us  [the longest x1 154 us: body(): pl.pallas_call(functools.partial(filter_kernel, R, C, both), out_shape=(f...]
where the time goes in v5:
time: 174 us; the launch traced here: 175 us
  Pallas kernels  167 us (96%)
  local copies, waits for them, and re-layouts  5.54 us (3%)
  between operations  1.97 us (1%)
    pallas_call x1, Pallas kernels, body(): pl.pallas_call(functools.partial(filter_kernel, R, C, both), out_shape=(f...  154 us
    pallas_call x2, Pallas kernels, build_panel(): pl.pallas_call(functools.partial(build_kernel, slots, panel_cols, tile, f...  13.2 us
    unnamed x12, local copies, waits for them, and re-layouts  5.54 us

profile of v5, /device:TPU:6, one launch (start us, length us, event | category | flops | bytes accessed | tf_op | source)
XLA Modules:
  0.0 174.5 jit_solution(7750511203049590317)
XLA Ops:
  1.9 0.0 copy-start
  1.9 2.3 %copy-done = bf16[1,48,192,192]{3,2,1,0:T(8,128)(2,1)S(1)} copy-done((bf16[1,48,192,192]{3,2,1,0:T(8,128)(2,1)S(1)}, bf16[1,48,192,192]{3,2,1,0:T(8,128)(2,1)}, u32[]{:S(2)}) %copy-start) | copy-done | bytes 3538968
  4.3 0.0 copy-start.2
  4.3 0.7 copy-done.2
  4.9 0.0 copy-start.3
  4.9 0.7 copy-done.3
  5.6 0.0 copy-start.4
  5.6 0.7 copy-done.4
  6.2 7.5 %shard_map.87.flipped_ref = bf16[1536,3072]{1,0:T(8,128)(2,1)S(1)} custom-call(s32[48]{0:T(128)S(1)} %bitcast.8, s32[48]{0:T(128)S(1)} %bitcast.6, s32[48]{0:T(128)S(1)} %bitcast.10, bf16[48,192,192]{2,1,0:T(8,128)(2,1)S(1)} %bitcast.4), custom_call_target="tpu_custom_call" | custom-call | tf_op jit(solution)/shard_map/pallas_call | solution.py:71
  13.8 0.0 copy-start.1
  13.8 5.7 %shard_map.86.panel_ref = bf16[3072,1536]{1,0:T(8,128)(2,1)S(1)} custom-call(s32[48]{0:T(128)S(1)} %bitcast.7, s32[48]{0:T(128)S(1)} %bitcast.9, s32[48]{0:T(128)S(1)} %bitcast.11, bf16[48,192,192]{2,1,0:T(8,128)(2,1)S(1)} %bitcast.5), custom_call_target="tpu_custom_call" | custom-call | tf_op jit(solution)/shard_map/pallas_call | solution.py:71
  19.4 0.0 copy-done.1
  19.4 153.8 %shard_map.88 = (f32[32,384]{1,0:T(8,128)S(1)}, f32[32,384]{1,0:T(8,128)S(1)}) custom-call(bf16[3072,1536]{1,0:T(8,128)(2,1)S(1)} %shard_map.86.panel_ref, bf16[1536,3072]{1,0:T(8,128)(2,1)S(1)} %shard_map.87.flipped_ref, f32[32,384]{1,0:T(8,128)S(1)} %copy-done.1, f32[1]{0:T(128)S(6)} %copy.11.center_ref, f32[1]{0:T(128)S(6)} %copy.12.half_ref), custom_call_target="tpu_custom_call" | custom-call | tf_op jit(solution)/shard_map/pallas_call | solution.py:373
  173.3 0.6 copy.13
  173.9 0.6 copy.14
Async XLA Ops:
  1.9 2.3 %copy-start = (bf16[1,48,192,192]{3,2,1,0:T(8,128)(2,1)S(1)}, bf16[1,48,192,192]{3,2,1,0:T(8,128)(2,1)}, u32[]{:S(2)}) copy-start(bf16[1,48,192,192]{3,2,1,0:T(8,128)(2,1)} %param.10) | copy-start | bytes 10616836
  4.3 0.7 copy-start.2
  4.9 0.7 copy-start.3
  5.6 0.7 copy-start.4
  13.8 5.7 %copy-start.1 = (f32[32,384]{1,0:T(8,128)S(1)}, f32[32,384]{1,0:T(8,128)}, u32[]{:S(2)}) copy-start(f32[32,384]{1,0:T(8,128)} %start_ref.1) | copy-start | bytes 147460

commit v6 on v4

--- a/solution.py
+++ b/solution.py
@@ -85,7 +85,7 @@
 
 def filter_kernel(
     R, C, both, panel_ref, flipped_ref, start_ref, center_ref, half_ref, out_ref, prev_ref,
-    rowp, colp, sendr, sendc, sends, redr, redc, reds, mir, mine,
+    rowp, colp, sendr, sendc, sends, redr, redc, reds, mine,
     ps_row, ps_sib, ps_col, pr_row, pr_col, rs_row, rs_sib, rs_col, rr_row, rr_sib, rr_col,
 ):
     w = start_ref.shape[1]
@@ -97,10 +97,10 @@
     sib = c + 1 - 2 * core
     root_row = c * R // C
     off = c * R % C
-    is_root = r == root_row
-    not_root = r != root_row
     col_home = (r * C + c) // R
     col_slot = c % R
+    stays = col_home == c
+    leaves = col_home != c
 
     def row_of(d):
         return (r + d) % R
@@ -118,15 +118,19 @@
     pl.semaphore_signal(barrier, inc=1, device_id=(r, sib), device_id_type=MESH)
     for d in range(1, Z):
         pl.semaphore_signal(barrier, inc=1, device_id=(r, 2 * chip(d) + core), device_id_type=MESH)
-    for d in range(1, R):
-        pl.semaphore_signal(barrier, inc=1, device_id=(row_of(d), col_home), device_id_type=MESH)
-
-    @pl.when(not_root)
-    def _():
-        for i in range(R):
+    for d in range(R):
+
+        @pl.when(leaves | (d != 0))
+        def _(d=d):
+            pl.semaphore_signal(barrier, inc=1, device_id=(row_of(d), col_home), device_id_type=MESH)
+
+    for i in range(R):
+
+        @pl.when(leaves | (col_slot != i))
+        def _(i=i):
             pl.semaphore_signal(barrier, inc=1, device_id=(root_row, off + i), device_id_type=MESH)
 
-    pl.semaphore_wait(barrier, jnp.where(is_root, Z + R - 1, Z + 2 * R - 1))
+    pl.semaphore_wait(barrier, jnp.where(stays, Z + 2 * R - 2, Z + 2 * R))
 
     out_ref[...] = start_ref[...]
     prev_ref[...] = start_ref[...]
@@ -170,56 +174,40 @@
         for d in range(Z):
             s_sib(par, d).wait_send()
 
-        @pl.when(not_root)
-        def _():
-            for i in range(R):
+        for i in range(R):
+
+            @pl.when(leaves | (col_slot != i))
+            def _(i=i):
                 s_col(par, i).wait_send()
 
     def step(k, carry):
         par = k % 2
-        rowp[par, c] = out_ref[...].astype(BF)
-        p_sib(par, 0).start()
+        rounded = out_ref[...].astype(BF)
+        rowp[par, c] = rounded
+        for d in range(1, R):
+            p_col(par, d).start()
+
+        @pl.when(leaves)
+        def _():
+            p_col(par, 0).start()
+
+        @pl.when(stays)
+        def _():
+            colp[par, col_slot] = rounded
+
         for d in range(Z - 1, 0, -1):
             p_row(par, d).start()
-        for d in range(1, R):
-            p_col(par, d).start()
+        p_sib(par, 0).start()
 
         @pl.when(k > 0)
         def _():
             wait_sums_sent(1 - par)
 
-        def arrive(d):
-            p_in(par, 2 * chip(d) + core).wait_recv()
-            p_sib(par, d).start()
-
-        for d in range(Z):
-            zz = chip(d)
-            p_in(par, 2 * zz + 1 - core).wait_recv()
-            lhs = jnp.concatenate([rowp[par, 2 * zz], rowp[par, 2 * zz + 1]], axis=1)
-            part = jnp.dot(lhs, panel_ref[pl.ds(zz * w2, w2), :], preferred_element_type=F32)
-            for i in range(R // 2):
-                piece = part[:, i * w2 : (i + 1) * w2]
-                if d == 0:
-                    mir[i] = piece
-                else:
-                    mir[i] += piece
-            if d == 0:
-                arrive(1)
-            if d + 2 < Z:
-                arrive(d + 2)
-
-        @pl.when(not_root)
-        def _():
-            for i in range(R):
-                sendc[i] = mir[i // 2, :, (i % 2) * w : (i % 2 + 1) * w].astype(BF)
-                s_col(par, i).start()
-            for i in range(R):
+        for i in range(R):
+
+            @pl.when(leaves | (col_slot != i))
+            def _(i=i):
                 p_col_in(par, i).wait_recv()
-
-        @pl.when(is_root)
-        def _():
-            for i in range(R):
-                colp[par, i] = rowp[par, off + i]
 
         def pass_on(d):
             s_sib(par, d).wait_recv()
@@ -237,34 +225,68 @@
                     x_col, panel_ref[pl.ds(zz * w2, w2), :], (((1,), (1,)), ((), ())),
                     preferred_element_type=F32,
                 )
-            place = zz - off // 2
-            inside = is_root & (place >= 0) & (place < R // 2)
-            part = part + jnp.where(inside, mir[jnp.clip(place, 0, R // 2 - 1)], 0.0)
             left, right = part[:, :w], part[:, w:]
             sends[d] = jnp.where(core == 0, right, left)
             s_sib(par, d).start()
             mine[d] = jnp.where(core == 0, left, right)
-            if d + 1 < Z:
-                pass_on(d + 1)
+            if d == Z - 1:
+                for e in range(1, Z):
+                    p_in(par, 2 * chip(e) + core).wait_recv()
+                    p_sib(par, e).start()
+            if d + 2 < Z:
+                pass_on(d + 2)
+
+        total = None
+        for d in range(Z):
+            zz = chip(d)
+            p_in(par, 2 * zz + 1 - core).wait_recv()
+            lhs = jnp.concatenate([rowp[par, 2 * zz], rowp[par, 2 * zz + 1]], axis=1)
+            part = jnp.dot(lhs, panel_ref[pl.ds(zz * w2, w2), :], preferred_element_type=F32)
+            total = part if d == 0 else total + part
+            if d == 0:
+                pass_on(1)
+
+        for i in range(R):
+            sendc[i] = total[:, i * w : (i + 1) * w].astype(BF)
+
+            @pl.when(leaves | (col_slot != i))
+            def _(i=i):
+                s_col(par, i).start()
+
+        @pl.when(stays)
+        def _():
+            redc[par, r] = sendc[col_slot]
 
         s_sib(par, 0).wait_recv()
-        total = mine[0] + reds[par, 0]
-        for d in range(1, R):
-            s_col_in(par, row_of(d)).wait_recv()
-            total = total + redc[par, row_of(d)].astype(F32)
+        product = mine[0] + reds[par, 0]
         for d in range(1, Z):
             s_row_in(par, d).wait_recv()
-            total = total + redr[par, chip(d)].astype(F32)
+            product = product + redr[par, chip(d)].astype(F32)
+        for d in range(R):
+            if d == 0:
+
+                @pl.when(leaves)
+                def _():
+                    s_col_in(par, r).wait_recv()
+
+            else:
+                s_col_in(par, row_of(d)).wait_recv()
+            product = product + redc[par, row_of(d)].astype(F32)
 
         first = k == 0
         scale = jnp.where(first, 1.0, 2.0)
         keep = jnp.where(first, 0.0, 1.0)
         current = out_ref[...]
-        following = scale * (total - center_ref[0] * current) / half_ref[0] - keep * prev_ref[...]
+        following = scale * (product - center_ref[0] * current) / half_ref[0] - keep * prev_ref[...]
         prev_ref[...] = current
         out_ref[...] = following
         for d in range(1, R):
             p_col(par, d).wait_send()
+
+        @pl.when(leaves)
+        def _():
+            p_col(par, 0).wait_send()
+
         for d in range(1, Z):
             p_row(par, d).wait_send()
         for d in range(Z):
@@ -307,7 +329,6 @@
             pltpu.VMEM((2, Z, vectors, w), BF),
             pltpu.VMEM((2, R, vectors, w), BF),
             pltpu.VMEM((2, Z, vectors, w), F32),
-            pltpu.VMEM((R // 2, vectors, 2 * w), F32),
             pltpu.VMEM((Z, vectors, w), F32),
             dma((Z,)), dma((Z,)), dma((R,)), dma((2, C)), dma((2, R)),
             dma((Z,)), dma((Z,)), dma((R,)), dma((2, Z)), dma((2, Z)), dma((2, R)),

time: 145 us -> 176 us (1.21)
  the two profiles are of different devices: /device:TPU:6 before, /device:TPU:0 now
where the time goes in v6:
time: 176 us
  Pallas kernels  168 us (95%)
  local copies, waits for them, and re-layouts  5.54 us (3%)
  between operations  1.97 us (1%)
    pallas_call x1, Pallas kernels, body(): pl.pallas_call(functools.partial(filter_kernel, R, C, both), out_shape=(f...  153 us
    pallas_call x2, Pallas kernels, build_panel(): pl.pallas_call(functools.partial(build_kernel, slots, panel_cols, tile, f...  15.5 us
    unnamed x12, local copies, waits for them, and re-layouts  5.54 us

profile of v6, /device:TPU:0, one launch (start us, length us, event | category | flops | bytes accessed | tf_op | source)
XLA Modules:
  0.0 175.9 jit_solution(6313912475809482187)
XLA Ops:
  1.9 0.0 copy-start
  1.9 2.3 %copy-done = bf16[1,48,192,192]{3,2,1,0:T(8,128)(2,1)S(1)} copy-done((bf16[1,48,192,192]{3,2,1,0:T(8,128)(2,1)S(1)}, bf16[1,48,192,192]{3,2,1,0:T(8,128)(2,1)}, u32[]{:S(2)}) %copy-start) | copy-done | bytes 3538968
  4.3 0.0 copy-start.2
  4.3 0.7 copy-done.2
  4.9 0.0 copy-start.3
  4.9 0.7 copy-done.3
  5.6 0.0 copy-start.4
  5.6 0.7 copy-done.4
  6.2 9.3 %shard_map.87.flipped_ref = bf16[1536,3072]{1,0:T(8,128)(2,1)S(1)} custom-call(s32[48]{0:T(128)S(1)} %bitcast.8, s32[48]{0:T(128)S(1)} %bitcast.6, s32[48]{0:T(128)S(1)} %bitcast.10, bf16[48,192,192]{2,1,0:T(8,128)(2,1)S(1)} %bitcast.4), custom_call_target="tpu_custom_call" | custom-call | tf_op jit(solution)/shard_map/pallas_call | solution.py:71
  15.6 0.0 copy-start.1
  15.6 6.2 %shard_map.86.panel_ref = bf16[3072,1536]{1,0:T(8,128)(2,1)S(1)} custom-call(s32[48]{0:T(128)S(1)} %bitcast.7, s32[48]{0:T(128)S(1)} %bitcast.9, s32[48]{0:T(128)S(1)} %bitcast.11, bf16[48,192,192]{2,1,0:T(8,128)(2,1)S(1)} %bitcast.5), custom_call_target="tpu_custom_call" | custom-call | tf_op jit(solution)/shard_map/pallas_call | solution.py:71
  21.8 0.0 copy-done.1
  21.8 152.9 %shard_map.88 = (f32[32,384]{1,0:T(8,128)S(1)}, f32[32,384]{1,0:T(8,128)S(1)}) custom-call(bf16[3072,1536]{1,0:T(8,128)(2,1)S(1)} %shard_map.86.panel_ref, bf16[1536,3072]{1,0:T(8,128)(2,1)S(1)} %shard_map.87.flipped_ref, f32[32,384]{1,0:T(8,128)S(1)} %copy-done.1, f32[1]{0:T(128)S(6)} %copy.11.center_ref, f32[1]{0:T(128)S(6)} %copy.12.half_ref), custom_call_target="tpu_custom_call" | custom-call | tf_op jit(solution)/shard_map/pallas_call | solution.py:318
  174.7 0.6 copy.13
  175.3 0.6 copy.14
Async XLA Ops:
  1.9 2.3 %copy-start = (bf16[1,48,192,192]{3,2,1,0:T(8,128)(2,1)S(1)}, bf16[1,48,192,192]{3,2,1,0:T(8,128)(2,1)}, u32[]{:S(2)}) copy-start(bf16[1,48,192,192]{3,2,1,0:T(8,128)(2,1)} %param.10) | copy-start | bytes 10616836
  4.3 0.7 copy-start.2
  4.9 0.7 copy-start.3
  5.6 0.7 copy-start.4
  15.6 6.2 %copy-start.1 = (f32[32,384]{1,0:T(8,128)S(1)}, f32[32,384]{1,0:T(8,128)}, u32[]{:S(2)}) copy-start(f32[32,384]{1,0:T(8,128)} %start_ref.1) | copy-start | bytes 147460

commit v7 on v4

--- a/solution.py
+++ b/solution.py
@@ -14,15 +14,16 @@
 
 
 def build_kernel(slots, panel_cols, tile, flip, rows_ref, cols_ref, live_ref, tiles_ref, out_ref, head, link, acc):
-    block_row = pl.program_id(0)
+    per_step = out_ref.shape[0] // tile
+    step = pl.program_id(0)
 
     def load(s):
         wide = tiles_ref[s].astype(F32)
         return wide.T if flip else wide
 
-    @pl.when(block_row == 0)
+    @pl.when(step == 0)
     def _():
-        @pl.loop(0, pl.num_programs(0) * panel_cols)
+        @pl.loop(0, pl.num_programs(0) * per_step * panel_cols)
         def _(b):
             head[b] = -1
 
@@ -34,52 +35,57 @@
                 link[s] = head[b]
                 head[b] = s
 
-    for pair in range(panel_cols // 2):
-        here = [head[block_row * panel_cols + 2 * pair + side] for side in range(2)]
-        empty = (here[0] < 0) & (here[1] < 0)
-        columns = slice(pair * 2 * tile, (pair + 1) * 2 * tile)
-
-        @pl.when(empty)
-        def _(columns=columns):
-            out_ref[:, columns] = jnp.zeros((tile, 2 * tile), BF)
-
-        @pl.when(jnp.logical_not(empty))
-        def _(columns=columns, here=here):
-            for side, s in enumerate(here):
-
-                @pl.when(s < 0)
-                def _(side=side):
-                    acc[side] = jnp.zeros((tile, tile), F32)
-
-                @pl.when(s >= 0)
-                def _(side=side, s=s):
-                    acc[side] = load(s)
-
-                    def more(t):
-                        acc[side] += load(t)
-                        return link[t]
-
-                    lax.while_loop(lambda t: t >= 0, more, link[s])
-
-            both = jnp.concatenate([acc[0], acc[1]], axis=1)
-            out_ref[:, columns] = both.astype(BF)
+    @pl.loop(0, per_step)
+    def _(local):
+        block_row = step * per_step + local
+        rows = pl.ds(pl.multiple_of(local * tile, tile), tile)
+        for pair in range(panel_cols // 2):
+            here = [head[block_row * panel_cols + 2 * pair + side] for side in range(2)]
+            empty = (here[0] < 0) & (here[1] < 0)
+            columns = slice(pair * 2 * tile, (pair + 1) * 2 * tile)
+
+            @pl.when(empty)
+            def _(columns=columns):
+                out_ref[rows, columns] = jnp.zeros((tile, 2 * tile), BF)
+
+            @pl.when(jnp.logical_not(empty))
+            def _(columns=columns, here=here):
+                for side, s in enumerate(here):
+
+                    @pl.when(s < 0)
+                    def _(side=side):
+                        acc[side] = jnp.zeros((tile, tile), F32)
+
+                    @pl.when(s >= 0)
+                    def _(side=side, s=s):
+                        acc[side] = load(s)
+
+                        def more(t):
+                            acc[side] += load(t)
+                            return link[t]
+
+                        lax.while_loop(lambda t: t >= 0, more, link[s])
+
+                both = jnp.concatenate([acc[0], acc[1]], axis=1)
+                out_ref[rows, columns] = both.astype(BF)
 
 
 def build_panel(tiles, row_ids, col_ids, live, panel_rows, panel_cols, flip=False):
     slots, tile, _ = tiles.shape
+    per_step = 4
     smem = pl.BlockSpec(memory_space=pltpu.SMEM)
     return pl.pallas_call(
         functools.partial(build_kernel, slots, panel_cols, tile, flip),
-        grid=(panel_rows,),
+        grid=(panel_rows // per_step,),
         out_shape=jax.ShapeDtypeStruct((panel_rows * tile, panel_cols * tile), BF),
         in_specs=[smem, smem, smem, pl.BlockSpec((slots, tile, tile), lambda i: (0, 0, 0))],
-        out_specs=pl.BlockSpec((tile, panel_cols * tile), lambda i: (i, 0)),
+        out_specs=pl.BlockSpec((per_step * tile, panel_cols * tile), lambda i: (i, 0)),
         scratch_shapes=[
             pltpu.SMEM((panel_rows * panel_cols,), jnp.int32),
             pltpu.SMEM((slots,), jnp.int32),
             pltpu.VMEM((2, tile, tile), F32),
         ],
-        compiler_params=pltpu.CompilerParams(vmem_limit_bytes=32 * 2**20),
+        compiler_params=pltpu.CompilerParams(vmem_limit_bytes=28 * 2**20),
     )(row_ids, col_ids, live, tiles)
 
 
@@ -244,8 +250,9 @@
             sends[d] = jnp.where(core == 0, right, left)
             s_sib(par, d).start()
             mine[d] = jnp.where(core == 0, left, right)
-            if d + 1 < Z:
-                pass_on(d + 1)
+            if d + 2 < Z:
+                pass_on(d + 2)
+        pass_on(1)
 
         s_sib(par, 0).wait_recv()
         total = mine[0] + reds[par, 0]

time: 145 us -> 142 us (0.979)
  Pallas kernels: 135 us -> 133 us
    pallas_call x1, Pallas kernels: 122 us -> 119 us  [body(): pl.pallas_call(functools.partial(filter_kernel, R, C, both), out_shape=(f...]
where the time goes in v7:
time: 142 us; the launch traced here: 140 us
  Pallas kernels  133 us (94%)
  local copies, waits for them, and re-layouts  5.54 us (4%)
  between operations  1.97 us (1%)
    pallas_call x1, Pallas kernels, body(): pl.pallas_call(functools.partial(filter_kernel, R, C, both), out_shape=(f...  119 us
    pallas_call x2, Pallas kernels, build_panel(): pl.pallas_call(functools.partial(build_kernel, slots, panel_cols, tile, f...  13.4 us
    unnamed x12, local copies, waits for them, and re-layouts  5.54 us

profile of v7, /device:TPU:6, one launch (start us, length us, event | category | flops | bytes accessed | tf_op | source)
XLA Modules:
  0.0 140.3 jit_solution(22347874497271366)
XLA Ops:
  1.9 0.0 copy-start
  1.9 2.3 %copy-done = bf16[1,48,192,192]{3,2,1,0:T(8,128)(2,1)S(1)} copy-done((bf16[1,48,192,192]{3,2,1,0:T(8,128)(2,1)S(1)}, bf16[1,48,192,192]{3,2,1,0:T(8,128)(2,1)}, u32[]{:S(2)}) %copy-start) | copy-done | bytes 3538968
  4.3 0.0 copy-start.2
  4.3 0.7 copy-done.2
  4.9 0.0 copy-start.3
  4.9 0.7 copy-done.3
  5.6 0.0 copy-start.4
  5.6 0.7 copy-done.4
  6.2 7.8 %shard_map.87.flipped_ref = bf16[1536,3072]{1,0:T(8,128)(2,1)S(1)} custom-call(s32[48]{0:T(128)S(1)} %bitcast.8, s32[48]{0:T(128)S(1)} %bitcast.6, s32[48]{0:T(128)S(1)} %bitcast.10, bf16[48,192,192]{2,1,0:T(8,128)(2,1)S(1)} %bitcast.4), custom_call_target="tpu_custom_call" | custom-call | tf_op jit(solution)/shard_map/pallas_call | solution.py:77
  14.1 0.0 copy-start.1
  14.1 5.5 %shard_map.86.panel_ref = bf16[3072,1536]{1,0:T(8,128)(2,1)S(1)} custom-call(s32[48]{0:T(128)S(1)} %bitcast.7, s32[48]{0:T(128)S(1)} %bitcast.9, s32[48]{0:T(128)S(1)} %bitcast.11, bf16[48,192,192]{2,1,0:T(8,128)(2,1)S(1)} %bitcast.5), custom_call_target="tpu_custom_call" | custom-call | tf_op jit(solution)/shard_map/pallas_call | solution.py:77
  19.6 0.0 copy-done.1
  19.6 119.4 %shard_map.88 = (f32[32,384]{1,0:T(8,128)S(1)}, f32[32,384]{1,0:T(8,128)S(1)}) custom-call(bf16[3072,1536]{1,0:T(8,128)(2,1)S(1)} %shard_map.86.panel_ref, bf16[1536,3072]{1,0:T(8,128)(2,1)S(1)} %shard_map.87.flipped_ref, f32[32,384]{1,0:T(8,128)S(1)} %copy-done.1, f32[1]{0:T(128)S(6)} %copy.11.center_ref, f32[1]{0:T(128)S(6)} %copy.12.half_ref), custom_call_target="tpu_custom_call" | custom-call | tf_op jit(solution)/shard_map/pallas_call | solution.py:303
  139.0 0.6 copy.13
  139.7 0.6 copy.14
Async XLA Ops:
  1.9 2.3 %copy-start = (bf16[1,48,192,192]{3,2,1,0:T(8,128)(2,1)S(1)}, bf16[1,48,192,192]{3,2,1,0:T(8,128)(2,1)}, u32[]{:S(2)}) copy-start(bf16[1,48,192,192]{3,2,1,0:T(8,128)(2,1)} %param.10) | copy-start | bytes 10616836
  4.3 0.7 copy-start.2
  4.9 0.7 copy-start.3
  5.6 0.7 copy-start.4
  14.1 5.5 %copy-start.1 = (f32[32,384]{1,0:T(8,128)S(1)}, f32[32,384]{1,0:T(8,128)}, u32[]{:S(2)}) copy-start(f32[32,384]{1,0:T(8,128)} %start_ref.1) | copy-start | bytes 147460

commit v8 on v7

--- a/solution.py
+++ b/solution.py
@@ -18,8 +18,8 @@
     step = pl.program_id(0)
 
     def load(s):
-        wide = tiles_ref[s].astype(F32)
-        return wide.T if flip else wide
+        block = tiles_ref[s]
+        return (block.T if flip else block).astype(F32)
 
     @pl.when(step == 0)
     def _():

time: 142 us -> 141 us (level)
  Pallas kernels: 133 us -> 131 us
    pallas_call x2, Pallas kernels: 13.4 us -> 11 us  [build_panel(): pl.pallas_call(functools.partial(build_kernel, slots, panel_cols, tile, f...]
where the time goes in v8:
time: 141 us; the launch traced here: 138 us
  Pallas kernels  131 us (93%)
  local copies, waits for them, and re-layouts  5.54 us (4%)
  between operations  1.97 us (1%)
    pallas_call x1, Pallas kernels, body(): pl.pallas_call(functools.partial(filter_kernel, R, C, both), out_shape=(f...  120 us
    pallas_call x2, Pallas kernels, build_panel(): pl.pallas_call(functools.partial(build_kernel, slots, panel_cols, tile, f...  11 us
    unnamed x12, local copies, waits for them, and re-layouts  5.54 us

profile of v8, /device:TPU:6, one launch (start us, length us, event | category | flops | bytes accessed | tf_op | source)
XLA Modules:
  0.0 138.4 jit_solution(8927256540786242159)
XLA Ops:
  1.9 0.0 copy-start
  1.9 2.3 %copy-done = bf16[1,48,192,192]{3,2,1,0:T(8,128)(2,1)S(1)} copy-done((bf16[1,48,192,192]{3,2,1,0:T(8,128)(2,1)S(1)}, bf16[1,48,192,192]{3,2,1,0:T(8,128)(2,1)}, u32[]{:S(2)}) %copy-start) | copy-done | bytes 3538968
  4.3 0.0 copy-start.2
  4.3 0.7 copy-done.2
  4.9 0.0 copy-start.3
  4.9 0.7 copy-done.3
  5.6 0.0 copy-start.4
  5.6 0.7 copy-done.4
  6.2 5.8 %shard_map.87.flipped_ref = bf16[1536,3072]{1,0:T(8,128)(2,1)S(1)} custom-call(s32[48]{0:T(128)S(1)} %bitcast.8, s32[48]{0:T(128)S(1)} %bitcast.6, s32[48]{0:T(128)S(1)} %bitcast.10, bf16[48,192,192]{2,1,0:T(8,128)(2,1)S(1)} %bitcast.4), custom_call_target="tpu_custom_call" | custom-call | tf_op jit(solution)/shard_map/pallas_call | solution.py:77
  12.1 0.0 copy-start.1
  12.1 5.2 %shard_map.86.panel_ref = bf16[3072,1536]{1,0:T(8,128)(2,1)S(1)} custom-call(s32[48]{0:T(128)S(1)} %bitcast.7, s32[48]{0:T(128)S(1)} %bitcast.9, s32[48]{0:T(128)S(1)} %bitcast.11, bf16[48,192,192]{2,1,0:T(8,128)(2,1)S(1)} %bitcast.5), custom_call_target="tpu_custom_call" | custom-call | tf_op jit(solution)/shard_map/pallas_call | solution.py:77
  17.3 0.0 copy-done.1
  17.3 119.8 %shard_map.88 = (f32[32,384]{1,0:T(8,128)S(1)}, f32[32,384]{1,0:T(8,128)S(1)}) custom-call(bf16[3072,1536]{1,0:T(8,128)(2,1)S(1)} %shard_map.86.panel_ref, bf16[1536,3072]{1,0:T(8,128)(2,1)S(1)} %shard_map.87.flipped_ref, f32[32,384]{1,0:T(8,128)S(1)} %copy-done.1, f32[1]{0:T(128)S(6)} %copy.11.center_ref, f32[1]{0:T(128)S(6)} %copy.12.half_ref), custom_call_target="tpu_custom_call" | custom-call | tf_op jit(solution)/shard_map/pallas_call | solution.py:303
  137.1 0.6 copy.13
  137.8 0.6 copy.14
Async XLA Ops:
  1.9 2.3 %copy-start = (bf16[1,48,192,192]{3,2,1,0:T(8,128)(2,1)S(1)}, bf16[1,48,192,192]{3,2,1,0:T(8,128)(2,1)}, u32[]{:S(2)}) copy-start(bf16[1,48,192,192]{3,2,1,0:T(8,128)(2,1)} %param.10) | copy-start | bytes 10616836
  4.3 0.7 copy-start.2
  4.9 0.7 copy-start.3
  5.6 0.7 copy-start.4
  12.1 5.2 %copy-start.1 = (f32[32,384]{1,0:T(8,128)S(1)}, f32[32,384]{1,0:T(8,128)}, u32[]{:S(2)}) copy-start(f32[32,384]{1,0:T(8,128)} %start_ref.1) | copy-start | bytes 147460
